TPU v7x, 512 devices: a whole 4x4x16 slice. The times are simulated.
512 devices in a mesh: cube: 128 (over z, y, core), row: 4 (over x).
Axes of the slice: x: 4, y: 4, z: 16, core: 2. Of those that a mesh axis runs over, the one named last changes fastest.
Arguments:
- fronts: bfloat16 [128, 256, 16384], P('cube', None, 'row'), may hold values from -0.046875 to 0.046875
- omega: bfloat16 [128, 16384, 256], P('cube', 'row'), may hold values from -6 to 6
- leaf_sizes: int32 [128], P('cube'), may hold values from 64 to 256, as said below
- leaf_map: int32 [128, 256], P('cube'), may hold values from 0 to 511, as said below
- own_one: bfloat16 [128, 256, 256], P('cube', 'row'), may hold values from -6 to 6
- parent_count: int32 [128], P('cube'), may hold values from 64 to 256, as said below
- parent_map: int32 [128, 256], P('cube'), may hold values from 0 to 1023, as said below
- own_two: bfloat16 [128, 256, 256], P('cube', 'row'), may hold values from -6 to 6
Outputs:
- level_one: bfloat16 [128, 256, 256], P('cube', 'row')
- level_two: bfloat16 [128, 256, 256], P('cube', 'row')
Inputs may be any that keep to these rules, and one draw needn't show every extreme that they name: `leaf_sizes`: some leaf has all 256 rows live. `leaf_map`: the rows of one leaf map to distinct parent rows. `parent_count`: some half has all 256 rows live. `parent_map`: the 512 rows of one level-one parent map to distinct level-two rows.
All inputs are finite; a program needn't handle non-finite values.
Results may differ from a plain program's by a relative error of at most 0.0039.
Values may be sent and summed in bfloat16 or wider, within the bound.
No kernel may reach another device: no remote copies, remote signals or barrier semaphores. Data moves between devices by JAX's collectives and lax.ppermute only.
A program may use at most 64 MiB of HBM per device.

v0:
```python
import jax
import jax.numpy as jnp
from jax import lax
from jax.sharding import PartitionSpec as P


def from_partner(block, axis, bit):
    count = lax.axis_size(axis)
    route = []
    for low in range(count):
        high = low | 1 << bit
        if high != low and high < count:
            route += [(low, high), (high, low)]
    return lax.ppermute(block, axis, route)


def by_rows(values, targets, levels, own):
    block = own.shape[0]
    n_row = lax.axis_size("row")
    gathered, indices = (
        lax.all_gather(values, "row", axis=0, tiled=True),
        lax.all_gather(targets, "row", axis=0, tiled=True),
    )
    for bit in range(levels):
        peer_rows, peer_index = from_partner((gathered, indices), "cube", bit)
        gathered = jnp.concatenate([gathered, peer_rows], axis=0)
        indices = jnp.concatenate([indices, peer_index], axis=0)
    group = 2**levels
    first = lax.axis_index("cube") % group * (block * n_row) + lax.axis_index("row") * block
    wanted = first + jnp.arange(block, dtype=jnp.int32)
    select = (indices[None, :] == wanted[:, None]).astype(jnp.bfloat16)
    summed = jnp.dot(select, gathered, preferred_element_type=jnp.float32)
    return (summed + own.astype(jnp.float32)).astype(jnp.bfloat16)


def assemble(values, targets, levels, own):
    return by_rows(values, targets, levels, own)


def body(fronts, omega, leaf_sizes, leaf_map, own_one, parent_count, parent_map, own_two):
    n_row = lax.axis_size("row")
    position = lax.axis_index("row")
    block_rows = fronts.shape[1] // n_row
    front_rows = fronts[0]
    sample_cols = omega[0]
    leaf_part = lax.psum_scatter(
        jnp.dot(front_rows, sample_cols, preferred_element_type=jnp.float32),
        "row",
        scatter_dimension=0,
        tiled=True,
    )
    samples = leaf_part.astype(jnp.bfloat16)
    local_rows = position * block_rows + jnp.arange(block_rows, dtype=jnp.int32)
    leaf_target = lax.dynamic_slice_in_dim(leaf_map[0], position * block_rows, block_rows, 0)
    leaf_target = jnp.where(local_rows < leaf_sizes[0], leaf_target, -1)
    level_one = assemble(samples, leaf_target, 1, own_one[0])
    half_rows = own_one.shape[1]
    half_local = position * half_rows + jnp.arange(half_rows, dtype=jnp.int32)
    upper_target = lax.dynamic_slice_in_dim(parent_map[0], position * half_rows, half_rows, 0)
    upper_target = jnp.where(half_local < parent_count[0], upper_target, -1)
    level_two = assemble(level_one, upper_target, 2, own_two[0])
    return (level_one[None], level_two[None])


def solution(mesh):
    in_specs = (
        P("cube", None, "row"),
        P("cube", "row", None),
        P("cube"),
        P("cube", None),
        P("cube", "row", None),
        P("cube"),
        P("cube", None),
        P("cube", "row", None),
    )
    out_specs = (P("cube", "row", None), P("cube", "row", None))
    return jax.shard_map(body, mesh=mesh, in_specs=in_specs, out_specs=out_specs, check_vma=False)
```

profile of v0, /device:TPU:1, one launch (start us, length us, event | category | flops | bytes accessed | tf_op | source)
XLA Modules:
  0.0 95.4 jit_solution(13474536413022864634)
XLA Ops:
  7.2 0.0 copy-start
  7.2 0.0 copy-start.2
  7.2 0.0 copy-start.3
  7.2 0.0 copy-start.4
  7.2 0.0 copy-start.5
  7.2 0.0 reduce-scatter.2.cloned.1.call-start
  7.3 1.5 %copy-done = bf16[1,4096,256]{2,1,0:T(8,128)(2,1)S(1)} copy-done((bf16[1,4096,256]{2,1,0:T(8,128)(2,1)S(1)}, bf16[1,4096,256]{2,1,0:T(8,128)(2,1)}, u32[]{:S(2)}) %copy-start) | copy-done | bytes 2097176
  8.8 3.0 %fusion = f32[256,256]{1,0:T(8,128)} fusion(bf16[1,4096,256]{2,1,0:T(8,128)(2,1)S(1)} %copy-done, bf16[1,256,4096]{2,1,0:T(8,128)(2,1)} %param.8), kind=kOutput, calls=%fused_computation | convolution fusion | flops 536870912 | bytes 4456448 | tf_op jit(solution)/shard_map/dot_general | solution.py:47
  11.8 0.0 reduce-scatter.2.cloned.1.call-update
  13.1 1.3 %dynamic-slice.2 = u32[1]{0:T(128)} dynamic-slice(u32[512]{0:T(512)} %constant.51, u32[]{:T(128)S(6)} %add.66), dynamic_slice_sizes={1} | dynamic-slice | bytes 12
  15.0 0.0 copy-done.2
  15.0 0.2 fusion.20
  15.2 0.2 fusion.21
  15.4 7.7 %all-reduce.2 = (s32[256]{0:T(256)S(1)}, s32[256]{0:T(256)S(1)}) all-reduce(s32[256]{0:T(256)S(1)} %fusion.20, s32[256]{0:T(256)S(1)} %fusion.21), channel_id=1, replica_groups=mesh['cube'=128,'row'=4] {'row'}, use_global_device_ids=true, to_apply=%add | all-reduce | flops 512 | bytes 4096
  23.1 6.8 %collective-permute-start = (s32[256]{0:T(256)S(1)}, s32[256]{0:T(256)S(1)}, u32[]{:S(2)}, u32[]{:S(2)}) collective-permute-start(s32[256]{0:T(256)S(1)} %get-tuple-element.2), channel_id=1, source_target_pairs={{0,4},{4,0},{8,12},{12,8},{16,20},{20,16},{24,28},{28,24},{32,36},... | collective-permute-start | bytes 3080 | tf_op jit(solution)/shard_map/ppermute | solution.py:14
  29.9 13.3 %reduce-scatter.2.cloned.1.call-done = f32[64,256]{1,0:T(8,128)} async-done(((f32[256,256]{1,0:T(8,128)}), f32[64,256]{1,0:T(8,128)}) %reduce-scatter.2.cloned.1.call-update) | async-done | bytes 65552 | tf_op jit(solution)/shard_map/reduce_scatter | solution.py:46
  43.3 0.8 convert_element_type.23
  44.1 9.1 %all_gather.13 = bf16[256,256]{1,0:T(8,128)(2,1)S(1)} all-gather(bf16[64,256]{1,0:T(8,128)(2,1)S(1)} %convert_element_type.23), channel_id=1, replica_groups=mesh['cube'=128,'row'=4] {'row'}, dimensions={0}, use_global_device_ids=true | all-gather | bytes 163840 | tf_op jit(solution)/shard_map/all_gather | solution.py:21
  53.2 7.7 %collective-permute-start.1 = (bf16[256,256]{1,0:T(8,128)(2,1)S(1)}, bf16[256,256]{1,0:T(8,128)(2,1)S(1)}, u32[]{:S(2)}, u32[]{:S(2)}) collective-permute-start(bf16[256,256]{1,0:T(8,128)(2,1)S(1)} %all_gather.13), channel_id=1, source_target_pairs={{0,4},{4,0},{8,12},{12,8},{16,20},{20,16},{24,28},{28,24},{32,36},... | collective-permute-start | bytes 393224 | tf_op jit(solution)/shard_map/ppermute | solution.py:14
  60.9 0.0 collective-permute-done
  60.9 0.9 collective-permute-done.1
  61.8 0.2 fusion.4
  62.1 9.1 %all_gather.15 = bf16[256,256]{1,0:T(8,128)(2,1)S(1)} all-gather(bf16[64,256]{1,0:T(8,128)(2,1)S(1)} %fusion.4), channel_id=1, replica_groups=mesh['cube'=128,'row'=4] {'row'}, dimensions={0}, use_global_device_ids=true | all-gather | bytes 163840 | tf_op jit(solution)/shard_map/all_gather | solution.py:21
  71.2 5.1 %collective-permute-start.4 = (bf16[256,256]{1,0:T(8,128)(2,1)S(1)}, bf16[256,256]{1,0:T(8,128)(2,1)S(1)}, u32[]{:S(2)}, u32[]{:S(2)}) collective-permute-start(bf16[256,256]{1,0:T(8,128)(2,1)S(1)} %all_gather.15), channel_id=1, source_target_pairs={{0,4},{4,0},{8,12},{12,8},{16,20},{20,16},{24,28},{28,24},{32,36},... | collective-permute-start | bytes 393224 | tf_op jit(solution)/shard_map/ppermute | solution.py:14
  76.3 1.9 %collective-permute-start.2 = (s32[256]{0:T(256)S(1)}, s32[256]{0:T(256)S(1)}, u32[]{:S(2)}, u32[]{:S(2)}) collective-permute-start(s32[256]{0:T(256)S(1)} %get-tuple-element.3), channel_id=1, source_target_pairs={{0,4},{4,0},{8,12},{12,8},{16,20},{20,16},{24,28},{28,24},{32,36},... | collective-permute-start | bytes 3080 | tf_op jit(solution)/shard_map/ppermute | solution.py:14
  78.3 0.0 collective-permute-done.4
  78.3 3.2 %collective-permute-start.5 = (bf16[512,256]{1,0:T(8,128)(2,1)S(1)}, bf16[512,256]{1,0:T(8,128)(2,1)S(1)}, u32[]{:S(2)}, u32[]{:S(2)}) collective-permute-start(bf16[512,256]{1,0:T(8,128)(2,1)S(1)} %pad_maximum_fusion), channel_id=1, source_target_pairs={{0,8},{8,0},{4,12},{12,4},{16,24},{24,16},{20,28},{28,20},{32,40},... | collective-permute-start | bytes 786440 | tf_op jit(solution)/shard_map/ppermute | solution.py:14
  81.5 0.0 collective-permute-done.2
  81.5 2.1 %collective-permute-start.3 = (s32[512]{0:T(512)S(1)}, s32[512]{0:T(512)S(1)}, u32[]{:S(2)}, u32[]{:S(2)}) collective-permute-start(s32[512]{0:T(512)S(1)} %pad_add_fusion.2), channel_id=1, source_target_pairs={{0,8},{8,0},{4,12},{12,4},{16,24},{24,16},{20,28},{28,20},{32,40},... | collective-permute-start | bytes 6152 | tf_op jit(solution)/shard_map/ppermute | solution.py:14
  83.7 4.0 %collective-permute-done.3 = s32[512]{0:T(512)S(1)} collective-permute-done((s32[512]{0:T(512)S(1)}, s32[512]{0:T(512)S(1)}, u32[]{:S(2)}, u32[]{:S(2)}) %collective-permute-start.3) | collective-permute-done | bytes 2080 | tf_op jit(solution)/shard_map/ppermute | solution.py:14
  87.6 0.0 collective-permute-done.5
  87.7 0.9 fusion.5
  (13 shorter events, 0.1 us)
Async XLA Ops:
  7.2 1.6 %copy-start = (bf16[1,4096,256]{2,1,0:T(8,128)(2,1)S(1)}, bf16[1,4096,256]{2,1,0:T(8,128)(2,1)}, u32[]{:S(2)}) copy-start(bf16[1,4096,256]{2,1,0:T(8,128)(2,1)} %param.9) | copy-start | bytes 6291460
  7.2 7.9 %copy-start.2 = (s32[1,256]{1,0:T(1,128)S(1)}, s32[1,256]{1,0:T(1,128)}, u32[]{:S(2)}) copy-start(s32[1,256]{1,0:T(1,128)} %param.11) | copy-start | bytes 3076
  7.2 8.0 %copy-start.3 = (s32[1,256]{1,0:T(1,128)S(1)}, s32[1,256]{1,0:T(1,128)}, u32[]{:S(2)}) copy-start(s32[1,256]{1,0:T(1,128)} %param.14) | copy-start | bytes 3076
  7.2 54.6 %copy-start.4 = (bf16[1,64,256]{2,1,0:T(8,128)(2,1)S(1)}, bf16[1,64,256]{2,1,0:T(8,128)(2,1)}, u32[]{:S(2)}) copy-start(bf16[1,64,256]{2,1,0:T(8,128)(2,1)} %param.12) | copy-start | bytes 98308
  7.2 80.4 %copy-start.5 = (bf16[1,64,256]{2,1,0:T(8,128)(2,1)S(1)}, bf16[1,64,256]{2,1,0:T(8,128)(2,1)}, u32[]{:S(2)}) copy-start(bf16[1,64,256]{2,1,0:T(8,128)(2,1)} %param.15) | copy-start | bytes 98308
  7.2 36.0 %reduce-scatter.2.cloned.1.call-start = ((), (), s32[]{:S(2)}) async-start(), calls=%async_computation.1 | async-start | bytes 327680 | tf_op jit(solution)/shard_map/reduce_scatter | solution.py:46
  23.1 37.8 %collective-permute-start = (s32[256]{0:T(256)S(1)}, s32[256]{0:T(256)S(1)}, u32[]{:S(2)}, u32[]{:S(2)}) collective-permute-start(s32[256]{0:T(256)S(1)} %get-tuple-element.2), channel_id=1, source_target_pairs={{0,4},{4,0},{8,12},{12,8},{16,20},{20,16},{24,28},{28,24},{32,36},... | collective-permute-start | bytes 3080 | tf_op jit(solution)/shard_map/ppermute | solution.py:14
  53.2 8.6 %collective-permute-start.1 = (bf16[256,256]{1,0:T(8,128)(2,1)S(1)}, bf16[256,256]{1,0:T(8,128)(2,1)S(1)}, u32[]{:S(2)}, u32[]{:S(2)}) collective-permute-start(bf16[256,256]{1,0:T(8,128)(2,1)S(1)} %all_gather.13), channel_id=1, source_target_pairs={{0,4},{4,0},{8,12},{12,8},{16,20},{20,16},{24,28},{28,24},{32,36},... | collective-permute-start | bytes 393224 | tf_op jit(solution)/shard_map/ppermute | solution.py:14
  62.1 26.5 %copy-start.1 = (bf16[64,256]{1,0:T(8,128)(2,1)}, bf16[64,256]{1,0:T(8,128)(2,1)S(1)}, u32[]{:S(2)}) copy-start(bf16[64,256]{1,0:T(8,128)(2,1)S(1)} %fusion.4) | copy-start | bytes 98308
  71.2 7.1 %collective-permute-start.4 = (bf16[256,256]{1,0:T(8,128)(2,1)S(1)}, bf16[256,256]{1,0:T(8,128)(2,1)S(1)}, u32[]{:S(2)}, u32[]{:S(2)}) collective-permute-start(bf16[256,256]{1,0:T(8,128)(2,1)S(1)} %all_gather.15), channel_id=1, source_target_pairs={{0,4},{4,0},{8,12},{12,8},{16,20},{20,16},{24,28},{28,24},{32,36},... | collective-permute-start | bytes 393224 | tf_op jit(solution)/shard_map/ppermute | solution.py:14
  76.3 5.2 %collective-permute-start.2 = (s32[256]{0:T(256)S(1)}, s32[256]{0:T(256)S(1)}, u32[]{:S(2)}, u32[]{:S(2)}) collective-permute-start(s32[256]{0:T(256)S(1)} %get-tuple-element.3), channel_id=1, source_target_pairs={{0,4},{4,0},{8,12},{12,8},{16,20},{20,16},{24,28},{28,24},{32,36},... | collective-permute-start | bytes 3080 | tf_op jit(solution)/shard_map/ppermute | solution.py:14
  78.3 9.3 %collective-permute-start.5 = (bf16[512,256]{1,0:T(8,128)(2,1)S(1)}, bf16[512,256]{1,0:T(8,128)(2,1)S(1)}, u32[]{:S(2)}, u32[]{:S(2)}) collective-permute-start(bf16[512,256]{1,0:T(8,128)(2,1)S(1)} %pad_maximum_fusion), channel_id=1, source_target_pairs={{0,8},{8,0},{4,12},{12,4},{16,24},{24,16},{20,28},{28,20},{32,40},... | collective-permute-start | bytes 786440 | tf_op jit(solution)/shard_map/ppermute | solution.py:14
  81.5 6.1 %collective-permute-start.3 = (s32[512]{0:T(512)S(1)}, s32[512]{0:T(512)S(1)}, u32[]{:S(2)}, u32[]{:S(2)}) collective-permute-start(s32[512]{0:T(512)S(1)} %pad_add_fusion.2), channel_id=1, source_target_pairs={{0,8},{8,0},{4,12},{12,4},{16,24},{24,16},{20,28},{28,20},{32,40},... | collective-permute-start | bytes 6152 | tf_op jit(solution)/shard_map/ppermute | solution.py:14
Sparse Core Ops, SparseCore 0:
  11.9 31.3 reduce-scatter.1
where the time goes:
time: 95.8 us; the launch traced here: 95.4 us
  starting transfers between devices  26.9 us (28%)
  blocking collectives  25.9 us (27%)
  waiting for transfers between devices  18.3 us (19%)
  between operations  16.2 us (17%)
  matrix products  4.09 us (4%)
  local copies, waits for them, and re-layouts  2.8 us (3%)
  other arithmetic  1.23 us (1%)
    ppermute x6, starting transfers between devices, from_partner(): return lax.ppermute(block, axis, route)  26.9 us
    all_gather x2, blocking collectives, by_rows(): lax.all_gather(values, 'row', axis=0, tiled=True)  18.2 us
    reduce_scatter x1, waiting for transfers between devices, body(): lax.psum_scatter(jnp.dot(front_rows, sample_cols, preferred_element_type=...  13.3 us
    unnamed x1, blocking collectives  7.69 us
    ppermute x6, waiting for transfers between devices, from_partner(): return lax.ppermute(block, axis, route)  4.91 us
    dot_general x1, matrix products, body(): jnp.dot(front_rows, sample_cols, preferred_element_type=jnp.float32)  3.01 us
    unnamed x15, local copies, waits for them, and re-layouts  2.8 us
  transfers between devices with their start and end apart: 7, of which 3 were waited for; matrix products, arithmetic and copies ran while one was open for 3% of the time, Pallas kernels for 0%

commit v1 on v0

v1 whole, which is shorter than its diff:
```python
import jax
import jax.numpy as jnp
from jax import lax
from jax.experimental import pallas as pl
from jax.experimental.pallas import tpu as pltpu
from jax.sharding import Mesh, PartitionSpec as P

CHUNKS = 4
DIGIT = 32
CODE_ROWS = 16
LIMIT = 32 * 2**20


def whole(memory):
    return pl.BlockSpec(memory_space=memory)


def product_kernel(fronts, omega, own, leaf_map, parent_map, leaf_size, count, out, a, b, sems):
    depth = a.shape[1] // CHUNKS
    rows = a.shape[0]
    copies = []
    for k in range(CHUNKS):
        part = pl.ds(k * depth, depth)
        copies.append(
            (
                pltpu.make_async_copy(fronts.at[0, :, part], a.at[:, part], sems.at[0, k]),
                pltpu.make_async_copy(omega.at[0, part, :], b.at[part, :], sems.at[1, k]),
            )
        )
        for copy in copies[-1]:
            copy.start()
    place = lax.broadcasted_iota(jnp.int32, (1, rows), 1)
    leaf = jnp.where(place < leaf_size[0], leaf_map[...], -1)
    parent = jnp.where(place < count[0], parent_map[...], -1)
    line = lax.broadcasted_iota(jnp.int32, (CODE_ROWS, rows), 0)
    code = jnp.where(line < 2, leaf, parent)
    code = jnp.where(line % 2 == 0, code >> 5, code & (DIGIT - 1))
    mine = own.shape[1]
    out[rows : rows + mine, :] = own[0]
    out[rows + mine :, :] = code.astype(jnp.float32).astype(jnp.bfloat16)
    total = None
    for k in range(CHUNKS):
        part = pl.ds(k * depth, depth)
        for copy in copies[k]:
            copy.wait()
        term = jnp.dot(a[:, part], b[part, :], preferred_element_type=jnp.float32)
        total = term if total is None else total + term
    out[:rows, :] = total.astype(jnp.bfloat16)


def decode(code):
    digits = code.astype(jnp.float32)
    leaf = digits[0:1] * DIGIT + digits[1:2]
    parent = digits[2:3] * DIGIT + digits[3:4]
    return leaf.astype(jnp.int32), parent.astype(jnp.int32)


def place_kernel(mine, other, out, parents):
    rows = out.shape[2]
    block = out.shape[1] // 2
    n_row = rows // block
    core, row = lax.axis_index("core"), lax.axis_index("row")
    leaf_a, parent_a = decode(mine[rows + block :, :])
    leaf_b, parent_b = decode(other[rows + block :, :])
    line = lax.broadcasted_iota(jnp.int32, (2 * rows, rows), 0)
    parent_row = jnp.bitwise_xor(line, core * rows)
    pick_a = (parent_row == leaf_a).astype(jnp.bfloat16)
    pick_b = (parent_row == leaf_b).astype(jnp.bfloat16)
    summed = jnp.dot(pick_a, mine[:rows, :], preferred_element_type=jnp.float32)
    summed += jnp.dot(pick_b, other[:rows, :], preferred_element_type=jnp.float32)
    level_one = summed[:rows].astype(jnp.bfloat16)
    for y in range(2):
        for x in range(n_row):
            out[y * n_row + x, block:, :] = level_one[x * block : (x + 1) * block]
    parents[...] = summed
    first = pl.multiple_of(row * block, block)
    parents[pl.ds(first, block), :] += mine[rows : rows + block, :].astype(jnp.float32)
    parents[pl.ds(rows + first, block), :] += other[rows : rows + block, :].astype(jnp.float32)
    quarter = jnp.where(line < rows, line, line + rows) + core * rows
    pick_a = (quarter == parent_a).astype(jnp.bfloat16)
    pick_b = (quarter == parent_b).astype(jnp.bfloat16)
    upper = jnp.dot(pick_a, parents[:rows].astype(jnp.bfloat16), preferred_element_type=jnp.float32)
    upper += jnp.dot(pick_b, parents[rows:].astype(jnp.bfloat16), preferred_element_type=jnp.float32)
    upper = upper.astype(jnp.bfloat16)
    for k in range(2 * n_row):
        out[k, :block, :] = upper[k * block : (k + 1) * block]


def sum_kernel(pieces, own_one, own_two, one, two):
    n_row = pieces.shape[0] // 2
    block = own_one.shape[1]
    first = lax.axis_index("y") * n_row
    total = own_one[0].astype(jnp.float32)
    for x in range(n_row):
        total += pieces[first + x, block:, :].astype(jnp.float32)
    one[0] = total.astype(jnp.bfloat16)
    total = own_two[0].astype(jnp.float32)
    for k in range(2 * n_row):
        total += pieces[k, :block, :].astype(jnp.float32)
    two[0] = total.astype(jnp.bfloat16)


def body(fronts, omega, leaf_sizes, leaf_map, own_one, parent_count, parent_map, own_two):
    _, rows, depth = fronts.shape
    cols = omega.shape[2]
    block = own_one.shape[1]
    params = pltpu.CompilerParams(vmem_limit_bytes=LIMIT)
    vmem, smem = whole(pltpu.VMEM), whole(pltpu.SMEM)
    hbm = lambda array: pltpu.with_memory_space_constraint(array, pltpu.HBM)
    near = lambda array: pltpu.with_memory_space_constraint(array, pltpu.VMEM)
    message = pl.pallas_call(
        product_kernel,
        out_shape=pltpu.VMEM((rows + block + CODE_ROWS, cols), jnp.bfloat16),
        in_specs=[whole(pl.ANY), whole(pl.ANY), vmem, vmem, vmem, smem, smem],
        out_specs=vmem,
        scratch_shapes=[
            pltpu.VMEM((rows, depth), jnp.bfloat16),
            pltpu.VMEM((depth, cols), jnp.bfloat16),
            pltpu.SemaphoreType.DMA((2, CHUNKS)),
        ],
        compiler_params=params,
        name="product",
    )(hbm(fronts), hbm(omega), own_one, leaf_map, parent_map, leaf_sizes, parent_count)
    sibling = lax.ppermute(message, "core", [(0, 1), (1, 0)])
    n_row = rows // block
    pieces = pl.pallas_call(
        place_kernel,
        out_shape=pltpu.VMEM((2 * n_row, 2 * block, cols), jnp.bfloat16),
        in_specs=[vmem, vmem],
        out_specs=vmem,
        scratch_shapes=[pltpu.VMEM((2 * rows, cols), jnp.float32)],
        compiler_params=params,
        name="place",
    )(near(message), near(sibling))
    pieces = lax.all_to_all(pieces, ("y", "row"), 0, 0)
    shape = jax.ShapeDtypeStruct(own_one.shape, jnp.bfloat16)
    return pl.pallas_call(
        sum_kernel,
        out_shape=(shape, shape),
        in_specs=[vmem, vmem, vmem],
        out_specs=(vmem, vmem),
        compiler_params=params,
        name="total",
    )(near(pieces), own_one, own_two)


def solution(mesh):
    n_cube, n_row = mesh.devices.shape
    grouped = Mesh(mesh.devices.reshape(n_cube // 4, 2, 2, n_row), ("group", "y", "core", "row"))
    cube = ("group", "y", "core")
    in_specs = (
        P(cube, None, "row"),
        P(cube, "row", None),
        P(cube),
        P(cube, None),
        P(cube, "row", None),
        P(cube),
        P(cube, None),
        P(cube, "row", None),
    )
    out_specs = (P(cube, "row", None), P(cube, "row", None))
    return jax.shard_map(body, mesh=grouped, in_specs=in_specs, out_specs=out_specs, check_vma=False)
```

time: 95.8 us -> 31.4 us (0.33)
  starting transfers between devices: 26.9 us -> 8.79 us
  waiting for transfers between devices: 18.3 us -> 1.02 us
  between operations: 16.2 us -> 1.96 us
  blocking collectives: 25.9 us -> 12.6 us
  Pallas kernels: 0 us -> 4.55 us
  matrix products: 4.09 us -> 0 us
  other arithmetic: 1.23 us -> 0 us
    all_gather x2 -> x0, blocking collectives: 18.2 us -> none  [by_rows(): lax.all_gather(values, 'row', axis=0, tiled=True)]
    ppermute x6 -> x1, starting transfers between devices: 26.9 us -> 8.79 us  [body(): sibling = lax.ppermute(message, 'core', [(0, 1), (1, 0)])]
    reduce_scatter x1 -> x0, waiting for transfers between devices: 13.3 us -> none  [body(): lax.psum_scatter(jnp.dot(front_rows, sample_cols, preferred_element_type=...]
    all_to_all x0 -> x1, blocking collectives: none -> 12.6 us  [body(): pieces = lax.all_to_all(pieces, ('y', 'row'), 0, 0)]
    unnamed x1 -> x0, blocking collectives: 7.69 us -> none
    pallas_call x0 -> x3, Pallas kernels: none -> 4.55 us  [the longest x1 3.02 us: body(): pl.pallas_call(product_kernel, out_shape=pltpu.VMEM((rows + block + CODE_...]
    dot_general x3 -> x0, matrix products: 4.09 us -> none  [the longest x1 3.01 us: body(): jnp.dot(front_rows, sample_cols, preferred_element_type=jnp.float32)]
    ppermute x6 -> x1, waiting for transfers between devices: 4.91 us -> 1.02 us  [body(): sibling = lax.ppermute(message, 'core', [(0, 1), (1, 0)])]
  transfers between devices with their start and end apart: 7 -> 1, of which waited for: 3 -> 1; matrix products, arithmetic and copies ran while one was open for 3% -> 0% of each run, Pallas kernels for 0% -> 0%
where the time goes in v1:
time: 31.4 us; the launch traced here: 31.1 us
  blocking collectives  12.6 us (40%)
  starting transfers between devices  8.79 us (28%)
  Pallas kernels  4.55 us (14%)
  local copies, waits for them, and re-layouts  2.12 us (7%)
  between operations  1.96 us (6%)
  waiting for transfers between devices  1.02 us (3%)
    all_to_all x1, blocking collectives, body(): pieces = lax.all_to_all(pieces, ('y', 'row'), 0, 0)  12.6 us
    ppermute x1, starting transfers between devices, body(): sibling = lax.ppermute(message, 'core', [(0, 1), (1, 0)])  8.79 us
    pallas_call x1, Pallas kernels, body(): pl.pallas_call(product_kernel, out_shape=pltpu.VMEM((rows + block + CODE_...  3.02 us
    unnamed x10, local copies, waits for them, and re-layouts  2.12 us
    ppermute x1, waiting for transfers between devices, body(): sibling = lax.ppermute(message, 'core', [(0, 1), (1, 0)])  1.02 us
    pallas_call x1, Pallas kernels, body(): pl.pallas_call(place_kernel, out_shape=pltpu.VMEM((2 * n_row, 2 * block,...  0.86 us
    pallas_call x1, Pallas kernels, body(): pl.pallas_call(sum_kernel, out_shape=(shape, shape), in_specs=[vmem, vmem...  0.68 us
  transfers between devices with their start and end apart: 1, of which 1 were waited for; matrix products, arithmetic and copies ran while one was open for 0% of the time, Pallas kernels for 0%

profile of v1, /device:TPU:1, one launch (start us, length us, event | category | flops | bytes accessed | tf_op | source)
XLA Modules:
  0.0 31.1 jit_solution(13883796004173692558)
XLA Ops:
  1.9 0.0 copy-start
  1.9 0.7 %copy-done = bf16[1,64,256]{2,1,0:T(8,128)(2,1)S(1)} copy-done((bf16[1,64,256]{2,1,0:T(8,128)(2,1)S(1)}, bf16[1,64,256]{2,1,0:T(8,128)(2,1)}, u32[]{:S(2)}) %copy-start) | copy-done | bytes 32792
  2.7 0.0 copy-start.3
  2.7 0.7 %copy-done.3 = s32[1,256]{1,0:T(1,128)S(1)} copy-done((s32[1,256]{1,0:T(1,128)S(1)}, s32[1,256]{1,0:T(1,128)}, u32[]{:S(2)}) %copy-start.3) | copy-done | bytes 1048
  3.4 0.0 copy-start.4
  3.4 0.7 %copy-done.4 = s32[1,256]{1,0:T(1,128)S(1)} copy-done((s32[1,256]{1,0:T(1,128)S(1)}, s32[1,256]{1,0:T(1,128)}, u32[]{:S(2)}) %copy-start.4) | copy-done | bytes 1048
  4.0 0.0 copy-start.1
  4.0 0.0 copy-start.2
  4.0 3.0 %product.1.mine = bf16[336,256]{1,0:T(8,128)(2,1)S(1)} custom-call(bf16[1,256,4096]{2,1,0:T(8,128)(2,1)} %fronts.1, bf16[1,4096,256]{2,1,0:T(8,128)(2,1)} %omega.1, bf16[1,64,256]{2,1,0:T(8,128)(2,1)S(1)} %copy-done, s32[1,256]{1,0:T(1,128)S(1)} %copy-done.3, s32[1,256]{1,0:T(1,128)S(1)} %copy-done.4, s32[1]{0:T(128)S(6)} %copy.10.leaf_size, s32[1]{0:T(128)S(6)} %copy.11.count), custom_call_target="tpu_custom_call" | custom-call | tf_op jit(solution)/shard_map/product/pallas_call | solution.py:111
  7.1 8.8 %collective-permute-start = (bf16[336,256]{1,0:T(8,128)(2,1)S(1)}, bf16[336,256]{1,0:T(8,128)(2,1)S(1)}, u32[]{:S(2)}, u32[]{:S(2)}) collective-permute-start(bf16[336,256]{1,0:T(8,128)(2,1)S(1)} %product.1.mine), channel_id=1, source_target_pairs={{0,4},{4,0},{1,5},{5,1},{2,6},{6,2},{3,7},{7,3},{8,12},{12,8},{9,1... | collective-permute-start | bytes 516104 | tf_op jit(solution)/shard_map/ppermute | solution.py:124
  15.9 1.0 %collective-permute-done.other = bf16[336,256]{1,0:T(8,128)(2,1)S(1)} collective-permute-done((bf16[336,256]{1,0:T(8,128)(2,1)S(1)}, bf16[336,256]{1,0:T(8,128)(2,1)S(1)}, u32[]{:S(2)}, u32[]{:S(2)}) %collective-permute-start) | collective-permute-done | bytes 172064 | tf_op jit(solution)/shard_map/ppermute | solution.py:124
  16.9 0.9 %place.1 = bf16[8,128,256]{2,1,0:T(8,128)(2,1)S(1)} custom-call(bf16[336,256]{1,0:T(8,128)(2,1)S(1)} %product.1.mine, bf16[336,256]{1,0:T(8,128)(2,1)S(1)} %collective-permute-done.other), custom_call_target="tpu_custom_call" | custom-call | tf_op jit(solution)/shard_map/place/pallas_call | solution.py:126
  17.7 12.6 %all_to_all.5.pieces = bf16[8,128,256]{2,1,0:T(8,128)(2,1)S(1)} all-to-all(bf16[8,128,256]{2,1,0:T(8,128)(2,1)S(1)} %place.1), channel_id=1, replica_groups=mesh['group'=32,'y'=2,'core'=2,'row'=4] {'y','row'}, dimensions={0} | all-to-all | bytes 1048576 | tf_op jit(solution)/shard_map/all_to_all | solution.py:135
  30.4 0.0 copy-done.1
  30.4 0.0 copy-done.2
  30.4 0.7 %total.1 = (bf16[1,64,256]{2,1,0:T(8,128)(2,1)}, bf16[1,64,256]{2,1,0:T(8,128)(2,1)}) custom-call(bf16[8,128,256]{2,1,0:T(8,128)(2,1)S(1)} %all_to_all.5.pieces, bf16[1,64,256]{2,1,0:T(8,128)(2,1)S(1)} %copy-done.1, bf16[1,64,256]{2,1,0:T(8,128)(2,1)S(1)} %copy-done.2), custom_call_target="tpu_custom_call" | custom-call | tf_op jit(solution)/shard_map/total/pallas_call | solution.py:137
Async XLA Ops:
  1.9 0.8 %copy-start = (bf16[1,64,256]{2,1,0:T(8,128)(2,1)S(1)}, bf16[1,64,256]{2,1,0:T(8,128)(2,1)}, u32[]{:S(2)}) copy-start(bf16[1,64,256]{2,1,0:T(8,128)(2,1)} %own_one.1) | copy-start | bytes 98308
  2.7 0.7 %copy-start.3 = (s32[1,256]{1,0:T(1,128)S(1)}, s32[1,256]{1,0:T(1,128)}, u32[]{:S(2)}) copy-start(s32[1,256]{1,0:T(1,128)} %leaf_map.1) | copy-start | bytes 3076
  3.4 0.7 %copy-start.4 = (s32[1,256]{1,0:T(1,128)S(1)}, s32[1,256]{1,0:T(1,128)}, u32[]{:S(2)}) copy-start(s32[1,256]{1,0:T(1,128)} %parent_map.1) | copy-start | bytes 3076
  4.0 26.4 %copy-start.1 = (bf16[1,64,256]{2,1,0:T(8,128)(2,1)S(1)}, bf16[1,64,256]{2,1,0:T(8,128)(2,1)}, u32[]{:S(2)}) copy-start(bf16[1,64,256]{2,1,0:T(8,128)(2,1)} %own_one.1) | copy-start | bytes 98308
  4.0 26.4 %copy-start.2 = (bf16[1,64,256]{2,1,0:T(8,128)(2,1)S(1)}, bf16[1,64,256]{2,1,0:T(8,128)(2,1)}, u32[]{:S(2)}) copy-start(bf16[1,64,256]{2,1,0:T(8,128)(2,1)} %own_two.1) | copy-start | bytes 98308
  7.1 9.8 %collective-permute-start = (bf16[336,256]{1,0:T(8,128)(2,1)S(1)}, bf16[336,256]{1,0:T(8,128)(2,1)S(1)}, u32[]{:S(2)}, u32[]{:S(2)}) collective-permute-start(bf16[336,256]{1,0:T(8,128)(2,1)S(1)} %product.1.mine), channel_id=1, source_target_pairs={{0,4},{4,0},{1,5},{5,1},{2,6},{6,2},{3,7},{7,3},{8,12},{12,8},{9,1... | collective-permute-start | bytes 516104 | tf_op jit(solution)/shard_map/ppermute | solution.py:124

commit v2 on v1

v2 whole, which is shorter than its diff:
```python
import jax
import jax.numpy as jnp
from jax import lax
from jax.experimental import pallas as pl
from jax.experimental.pallas import tpu as pltpu
from jax.sharding import Mesh, PartitionSpec as P

CHUNKS = 4
DIGIT = 32
CODE_ROWS = 16
LIMIT = 32 * 2**20
COST = pl.CostEstimate(flops=8 * 10**9, bytes_accessed=2**24, transcendentals=0)


def whole(memory):
    return pl.BlockSpec(memory_space=memory)


def first_kernel(out):
    out[...] = jnp.zeros_like(out)


def product_kernel(blank, fronts, omega, own_one, own_two, leaf_map, parent_map, leaf_size, count, out, two):
    rows = fronts.shape[1]
    mine = own_one.shape[1]
    place = lax.broadcasted_iota(jnp.int32, (1, rows), 1)
    leaf = jnp.where(place < leaf_size[0], leaf_map[...], -1)
    parent = jnp.where(place < count[0], parent_map[...], -1)
    line = lax.broadcasted_iota(jnp.int32, (CODE_ROWS, rows), 0)
    code = jnp.where(line < 2, leaf, parent)
    code = jnp.where(line % 2 == 0, code >> 5, code & (DIGIT - 1))
    out[rows + mine :, :] = (code.astype(jnp.float32) + blank[...]).astype(jnp.bfloat16)
    out[rows : rows + mine, :] = own_one[0]
    two[...] = own_two[0]
    out[:rows, :] = jnp.dot(fronts[0], omega[0], preferred_element_type=jnp.float32).astype(jnp.bfloat16)


def decode(code):
    digits = code.astype(jnp.float32)
    leaf = digits[0:1] * DIGIT + digits[1:2]
    parent = digits[2:3] * DIGIT + digits[3:4]
    return leaf.astype(jnp.int32), parent.astype(jnp.int32)


def picks(blocks, index):
    rows = index.shape[1]
    line = lax.broadcasted_iota(jnp.int32, (rows, rows), 0)
    return jnp.concatenate([(line + block * rows == index).astype(jnp.bfloat16) for block in blocks], axis=0)


def own_place_kernel(mine, parents, upper):
    rows = parents.shape[0] // 2
    core = lax.axis_index("core")
    leaf, parent = decode(mine[mine.shape[0] - CODE_ROWS :, :])
    pick = picks((core, 1 - core), leaf)
    parents[...] = jnp.dot(pick, mine[:rows, :], preferred_element_type=jnp.float32).astype(jnp.bfloat16)
    upper[...] = picks((core, core + 2), parent)


def place_kernel(mine, other, placed, picked, out):
    rows = out.shape[2]
    block = out.shape[1] // 2
    n_row = rows // block
    core, row = lax.axis_index("core"), lax.axis_index("row")
    leaf, parent = decode(other[rows + block :, :])
    pick = picks((core, 1 - core), leaf)
    parents = jnp.dot(pick, other[:rows, :], preferred_element_type=jnp.float32) + placed[...].astype(jnp.float32)
    level_one = parents[:rows].astype(jnp.bfloat16)
    for x in range(n_row):
        out[x, block:, :] = level_one[x * block : (x + 1) * block]
        out[n_row + x, block:, :] = level_one[x * block : (x + 1) * block]
    line = lax.broadcasted_iota(jnp.int32, (rows, 1), 0) // block == row
    own = jnp.concatenate([mine[rows : rows + block, :]] * n_row, axis=0).astype(jnp.float32)
    lower = (parents[:rows] + jnp.where(line, own, 0.0)).astype(jnp.bfloat16)
    upper = jnp.dot(picked[...], lower, preferred_element_type=jnp.float32)
    own = jnp.concatenate([other[rows : rows + block, :]] * n_row, axis=0).astype(jnp.float32)
    lower = (parents[rows:] + jnp.where(line, own, 0.0)).astype(jnp.bfloat16)
    upper += jnp.dot(picks((core, core + 2), parent), lower, preferred_element_type=jnp.float32)
    upper = upper.astype(jnp.bfloat16)
    for k in range(2 * n_row):
        out[k, :block, :] = upper[k * block : (k + 1) * block]


def sum_kernel(pieces, message, own_two, one, two):
    n_row, rows = pieces.shape[0] // 2, pieces.shape[2]
    block = own_two.shape[0]
    first = lax.axis_index("y") * n_row
    total = message[rows : rows + block, :].astype(jnp.float32)
    for x in range(n_row):
        total += pieces[first + x, block:, :].astype(jnp.float32)
    one[0] = total.astype(jnp.bfloat16)
    total = own_two[...].astype(jnp.float32)
    for k in range(2 * n_row):
        total += pieces[k, :block, :].astype(jnp.float32)
    two[0] = total.astype(jnp.bfloat16)


def body(fronts, omega, leaf_sizes, leaf_map, own_one, parent_count, parent_map, own_two):
    _, rows, depth = fronts.shape
    cols = omega.shape[2]
    block = own_one.shape[1]
    params = pltpu.CompilerParams(vmem_limit_bytes=LIMIT)
    vmem, smem = whole(pltpu.VMEM), whole(pltpu.SMEM)
    hbm = lambda array: pltpu.with_memory_space_constraint(array, pltpu.HBM)
    near = lambda array: pltpu.with_memory_space_constraint(array, pltpu.VMEM)
    blank = pl.pallas_call(
        first_kernel,
        out_shape=pltpu.VMEM((CODE_ROWS, cols), jnp.float32),
        in_specs=[],
        out_specs=vmem,
        compiler_params=params,
        cost_estimate=COST,
        name="first",
    )()
    message, late = pl.pallas_call(
        product_kernel,
        out_shape=(pltpu.VMEM((rows + block + CODE_ROWS, cols), jnp.bfloat16), pltpu.VMEM((block, cols), jnp.bfloat16)),
        in_specs=[vmem] * 7 + [smem, smem],
        out_specs=(vmem, vmem),
        compiler_params=params,
        name="product",
    )(near(blank), fronts, omega, own_one, own_two, leaf_map, parent_map, leaf_sizes, parent_count)
    sibling = lax.ppermute(message, "core", [(0, 1), (1, 0)])
    n_row = rows // block
    placed, picked = pl.pallas_call(
        own_place_kernel,
        out_shape=(pltpu.VMEM((2 * rows, cols), jnp.bfloat16), pltpu.VMEM((2 * rows, rows), jnp.bfloat16)),
        in_specs=[vmem],
        out_specs=(vmem, vmem),
        compiler_params=params,
        cost_estimate=pl.CostEstimate(flops=4 * rows * rows * cols, bytes_accessed=2**20, transcendentals=0),
        name="own_place",
    )(near(message))
    pieces = pl.pallas_call(
        place_kernel,
        out_shape=pltpu.VMEM((2 * n_row, 2 * block, cols), jnp.bfloat16),
        in_specs=[vmem] * 4,
        out_specs=vmem,
        compiler_params=params,
        name="place",
    )(near(message), near(sibling), near(placed), near(picked))
    pieces = lax.all_to_all(pieces, ("y", "row"), 0, 0)
    shape = jax.ShapeDtypeStruct(own_one.shape, jnp.bfloat16)
    return pl.pallas_call(
        sum_kernel,
        out_shape=(shape, shape),
        in_specs=[vmem, vmem, vmem],
        out_specs=(vmem, vmem),
        compiler_params=params,
        name="total",
    )(near(pieces), near(message), near(late))


def solution(mesh):
    n_cube, n_row = mesh.devices.shape
    grouped = Mesh(mesh.devices.reshape(n_cube // 4, 2, 2, n_row), ("group", "y", "core", "row"))
    cube = ("group", "y", "core")
    in_specs = (
        P(cube, None, "row"),
        P(cube, "row", None),
        P(cube),
        P(cube, None),
        P(cube, "row", None),
        P(cube),
        P(cube, None),
        P(cube, "row", None),
    )
    out_specs = (P(cube, "row", None), P(cube, "row", None))
    return jax.shard_map(body, mesh=grouped, in_specs=in_specs, out_specs=out_specs, check_vma=False)
```

time: 31.4 us -> 27.6 us (0.88)
  Pallas kernels: 4.55 us -> 2.24 us
  local copies, waits for them, and re-layouts: 2.12 us -> 0.34 us
  between operations: 1.96 us -> 2.64 us
    pallas_call x1 -> x3, Pallas kernels: 3.02 us -> 0.94 us  [the longest x1 0.71 us: body(): pl.pallas_call(product_kernel, out_shape=(pltpu.VMEM((rows + block + CODE...]
    unnamed x10 -> x12, local copies, waits for them, and re-layouts: 2.12 us -> 0.34 us
  transfers between devices with their start and end apart: 1 -> 1, of which waited for: 1 -> 1; matrix products, arithmetic and copies ran while one was open for 0% -> 0% of each run, Pallas kernels for 0% -> 1%
where the time goes in v2:
time: 27.6 us; the launch traced here: 27.4 us
  blocking collectives  12.6 us (46%)
  starting transfers between devices  8.79 us (32%)
  between operations  2.64 us (10%)
  Pallas kernels  2.24 us (8%)
  waiting for transfers between devices  0.78 us (3%)
  local copies, waits for them, and re-layouts  0.34 us (1%)
    all_to_all x1, blocking collectives, body(): pieces = lax.all_to_all(pieces, ('y', 'row'), 0, 0)  12.6 us
    ppermute x1, starting transfers between devices, body(): sibling = lax.ppermute(message, 'core', [(0, 1), (1, 0)])  8.79 us
    ppermute x1, waiting for transfers between devices, body(): sibling = lax.ppermute(message, 'core', [(0, 1), (1, 0)])  0.78 us
    pallas_call x1, Pallas kernels, body(): pl.pallas_call(product_kernel, out_shape=(pltpu.VMEM((rows + block + CODE...  0.71 us
    pallas_call x1, Pallas kernels, body(): pl.pallas_call(sum_kernel, out_shape=(shape, shape), in_specs=[vmem, vmem...  0.68 us
    pallas_call x1, Pallas kernels, body(): pl.pallas_call(place_kernel, out_shape=pltpu.VMEM((2 * n_row, 2 * block,...  0.62 us
  transfers between devices with their start and end apart: 1, of which 1 were waited for; matrix products, arithmetic and copies ran while one was open for 0% of the time, Pallas kernels for 1%

profile of v2, /device:TPU:1, one launch (start us, length us, event | category | flops | bytes accessed | tf_op | source)
XLA Modules:
  0.0 27.4 jit_solution(5516020096894450774)
XLA Ops:
  0.6 0.0 copy-start.3
  0.6 0.0 copy-start.5
  0.7 0.0 copy-start.2
  0.7 0.0 copy-start.4
  0.7 0.0 copy-start.1
  0.7 0.0 copy-start
  2.6 0.0 copy-done.3
  2.6 0.0 copy-done.5
  2.6 0.0 copy-done.2
  2.6 0.0 copy-done.4
  2.6 0.0 copy-done.1
  2.6 0.3 %copy-done = bf16[1,256,4096]{2,1,0:T(8,128)(2,1)S(1)} copy-done((bf16[1,256,4096]{2,1,0:T(8,128)(2,1)S(1)}, bf16[1,256,4096]{2,1,0:T(8,128)(2,1)}, u32[]{:S(2)}) %copy-start) | copy-done | bytes 2097176
  3.0 0.7 %product.1 = (bf16[336,256]{1,0:T(8,128)(2,1)S(1)}, bf16[64,256]{1,0:T(8,128)(2,1)S(1)}) custom-call(f32[16,256]{1,0:T(8,128)S(1)} %first.1.blank, bf16[1,256,4096]{2,1,0:T(8,128)(2,1)S(1)} %copy-done, bf16[1,4096,256]{2,1,0:T(8,128)(2,1)S(1)} %copy-done.1, bf16[1,64,256]{2,1,0:T(8,128)(2,1)S(1)} %copy-done.2, bf16[1,64,256]{2,1,0:T(8,128)(2,1)S(1)} %copy-done.3, ...), custom_call_target="tpu_custom_call" | custom-call | tf_op jit(solution)/shard_map/product/pallas_call | solution.py:115
  3.7 8.8 %collective-permute-start = (bf16[336,256]{1,0:T(8,128)(2,1)S(1)}, bf16[336,256]{1,0:T(8,128)(2,1)S(1)}, u32[]{:S(2)}, u32[]{:S(2)}) collective-permute-start(bf16[336,256]{1,0:T(8,128)(2,1)S(1)} %get-tuple-element.6.mine.message), channel_id=1, source_target_pairs={{0,4},{4,0},{1,5},{5,1},{2,6},{6,2},{3,7},{7,3},{8,12},{12,8},{9,1... | collective-permute-start | bytes 516104 | tf_op jit(solution)/shard_map/ppermute | solution.py:123
  12.5 0.2 own_place.1
  12.7 0.8 %collective-permute-done.other = bf16[336,256]{1,0:T(8,128)(2,1)S(1)} collective-permute-done((bf16[336,256]{1,0:T(8,128)(2,1)S(1)}, bf16[336,256]{1,0:T(8,128)(2,1)S(1)}, u32[]{:S(2)}, u32[]{:S(2)}) %collective-permute-start) | collective-permute-done | bytes 172064 | tf_op jit(solution)/shard_map/ppermute | solution.py:123
  13.5 0.6 %place.1 = bf16[8,128,256]{2,1,0:T(8,128)(2,1)S(1)} custom-call(bf16[336,256]{1,0:T(8,128)(2,1)S(1)} %get-tuple-element.6.mine.message, bf16[336,256]{1,0:T(8,128)(2,1)S(1)} %collective-permute-done.other, bf16[512,256]{1,0:T(8,128)(2,1)S(1)} %get-tuple-element.7.placed, bf16[512,256]{1,0:T(8,128)(2,1)S(1)} %get-tuple-element.8.picked), custom_call_target="tpu_custom_call" | custom-call | tf_op jit(solution)/shard_map/place/pallas_call | solution.py:134
  14.1 12.6 %all_to_all.5.pieces = bf16[8,128,256]{2,1,0:T(8,128)(2,1)S(1)} all-to-all(bf16[8,128,256]{2,1,0:T(8,128)(2,1)S(1)} %place.1), channel_id=1, replica_groups=mesh['group'=32,'y'=2,'core'=2,'row'=4] {'y','row'}, dimensions={0} | all-to-all | bytes 1048576 | tf_op jit(solution)/shard_map/all_to_all | solution.py:142
  26.8 0.7 %total.1 = (bf16[1,64,256]{2,1,0:T(8,128)(2,1)}, bf16[1,64,256]{2,1,0:T(8,128)(2,1)}) custom-call(bf16[8,128,256]{2,1,0:T(8,128)(2,1)S(1)} %all_to_all.5.pieces, bf16[336,256]{1,0:T(8,128)(2,1)S(1)} %get-tuple-element.6.mine.message, bf16[64,256]{1,0:T(8,128)(2,1)S(1)} %get-tuple-element.9.own_two), custom_call_target="tpu_custom_call" | custom-call | tf_op jit(solution)/shard_map/total/pallas_call | solution.py:144
  (1 shorter events, 0.0 us)
Async XLA Ops:
  0.6 2.0 %copy-start.3 = (bf16[1,64,256]{2,1,0:T(8,128)(2,1)S(1)}, bf16[1,64,256]{2,1,0:T(8,128)(2,1)}, u32[]{:S(2)}) copy-start(bf16[1,64,256]{2,1,0:T(8,128)(2,1)} %own_two.1) | copy-start | bytes 98308
  0.6 2.0 %copy-start.5 = (s32[1,256]{1,0:T(1,128)S(1)}, s32[1,256]{1,0:T(1,128)}, u32[]{:S(2)}) copy-start(s32[1,256]{1,0:T(1,128)} %parent_map.1) | copy-start | bytes 3076
  0.7 2.0 %copy-start.2 = (bf16[1,64,256]{2,1,0:T(8,128)(2,1)S(1)}, bf16[1,64,256]{2,1,0:T(8,128)(2,1)}, u32[]{:S(2)}) copy-start(bf16[1,64,256]{2,1,0:T(8,128)(2,1)} %own_one.1) | copy-start | bytes 98308
  0.7 2.0 %copy-start.4 = (s32[1,256]{1,0:T(1,128)S(1)}, s32[1,256]{1,0:T(1,128)}, u32[]{:S(2)}) copy-start(s32[1,256]{1,0:T(1,128)} %leaf_map.1) | copy-start | bytes 3076
  0.7 2.0 %copy-start.1 = (bf16[1,4096,256]{2,1,0:T(8,128)(2,1)S(1)}, bf16[1,4096,256]{2,1,0:T(8,128)(2,1)}, u32[]{:S(2)}) copy-start(bf16[1,4096,256]{2,1,0:T(8,128)(2,1)} %omega.1) | copy-start | bytes 6291460
  0.7 2.3 %copy-start = (bf16[1,256,4096]{2,1,0:T(8,128)(2,1)S(1)}, bf16[1,256,4096]{2,1,0:T(8,128)(2,1)}, u32[]{:S(2)}) copy-start(bf16[1,256,4096]{2,1,0:T(8,128)(2,1)} %fronts.1) | copy-start | bytes 6291460
  3.7 9.8 %collective-permute-start = (bf16[336,256]{1,0:T(8,128)(2,1)S(1)}, bf16[336,256]{1,0:T(8,128)(2,1)S(1)}, u32[]{:S(2)}, u32[]{:S(2)}) collective-permute-start(bf16[336,256]{1,0:T(8,128)(2,1)S(1)} %get-tuple-element.6.mine.message), channel_id=1, source_target_pairs={{0,4},{4,0},{1,5},{5,1},{2,6},{6,2},{3,7},{7,3},{8,12},{12,8},{9,1... | collective-permute-start | bytes 516104 | tf_op jit(solution)/shard_map/ppermute | solution.py:123

commit v3 on v2

v3 whole, which is shorter than its diff:
```python
import jax
import jax.numpy as jnp
from jax import lax
from jax.experimental import pallas as pl
from jax.experimental.pallas import tpu as pltpu
from jax.sharding import Mesh, PartitionSpec as P

DIGIT = 32
CODE_ROWS = 16
LIMIT = 32 * 2**20


def whole(memory):
    return pl.BlockSpec(memory_space=memory)


def picks(blocks, index):
    rows = index.shape[1]
    line = lax.broadcasted_iota(jnp.int32, (rows, rows), 0)
    return jnp.concatenate([(line + block * rows == index).astype(jnp.bfloat16) for block in blocks], axis=0)


def first_kernel(out):
    out[...] = jnp.zeros_like(out)


def product_kernel(blank, fronts, omega, own_one, own_two, leaf_map, parent_map, leaf_size, count, out, two, lower, upper):
    rows = fronts.shape[1]
    mine = own_one.shape[1]
    core = lax.axis_index("core")
    place = lax.broadcasted_iota(jnp.int32, (1, rows), 1)
    leaf = jnp.where(place < leaf_size[0], leaf_map[...], -1)
    parent = jnp.where(place < count[0], parent_map[...], -1)
    line = lax.broadcasted_iota(jnp.int32, (CODE_ROWS, rows), 0)
    code = jnp.where(line < 2, leaf, parent)
    code = jnp.where(line % 2 == 0, code >> 5, code & (DIGIT - 1))
    out[rows + mine :, :] = (code.astype(jnp.float32) + blank[...]).astype(jnp.bfloat16)
    out[rows : rows + mine, :] = own_one[0]
    two[...] = own_two[0]
    lower[...] = picks((core, 1 - core), leaf)
    upper[...] = picks((core, core + 2), parent)
    out[:rows, :] = jnp.dot(fronts[0], omega[0], preferred_element_type=jnp.float32).astype(jnp.bfloat16)


def decode(code):
    digits = code.astype(jnp.float32)
    leaf = digits[0:1] * DIGIT + digits[1:2]
    parent = digits[2:3] * DIGIT + digits[3:4]
    return leaf.astype(jnp.int32), parent.astype(jnp.int32)


def place_kernel(mine, both, lower, upper, out):
    rows = out.shape[2]
    block = out.shape[1] // 2
    n_row = rows // block
    core, row = lax.axis_index("core"), lax.axis_index("row")
    other = both.at[1 - core]
    leaf, parent = decode(other[rows + block :, :])
    parents = jnp.dot(lower[...], mine[:rows, :], preferred_element_type=jnp.float32)
    parents += jnp.dot(picks((core, 1 - core), leaf), other[:rows, :], preferred_element_type=jnp.float32)
    level_one = parents[:rows].astype(jnp.bfloat16)
    for x in range(n_row):
        for y in range(2):
            out[2 * x + y, block:, :] = level_one[x * block : (x + 1) * block]
    line = lax.broadcasted_iota(jnp.int32, (rows, 1), 0) // block == row
    own = jnp.concatenate([mine[rows : rows + block, :]] * n_row, axis=0).astype(jnp.float32)
    half = (parents[:rows] + jnp.where(line, own, 0.0)).astype(jnp.bfloat16)
    placed = jnp.dot(upper[...], half, preferred_element_type=jnp.float32)
    own = jnp.concatenate([other[rows : rows + block, :]] * n_row, axis=0).astype(jnp.float32)
    half = (parents[rows:] + jnp.where(line, own, 0.0)).astype(jnp.bfloat16)
    placed += jnp.dot(picks((core, core + 2), parent), half, preferred_element_type=jnp.float32)
    placed = placed.astype(jnp.bfloat16)
    for x in range(n_row):
        for y in range(2):
            out[2 * x + y, :block, :] = placed[y * rows + x * block : y * rows + (x + 1) * block]


def sum_kernel(pieces, message, own_two, one, two):
    n_row, rows = pieces.shape[0] // 2, pieces.shape[2]
    block = own_two.shape[0]
    y = lax.axis_index("y")
    total = message[rows : rows + block, :].astype(jnp.float32)
    for x in range(n_row):
        total += pieces[2 * x + y, block:, :].astype(jnp.float32)
    one[0] = total.astype(jnp.bfloat16)
    total = own_two[...].astype(jnp.float32)
    for k in range(2 * n_row):
        total += pieces[k, :block, :].astype(jnp.float32)
    two[0] = total.astype(jnp.bfloat16)


def body(fronts, omega, leaf_sizes, leaf_map, own_one, parent_count, parent_map, own_two):
    _, rows, depth = fronts.shape
    cols = omega.shape[2]
    block = own_one.shape[1]
    n_row = rows // block
    params = pltpu.CompilerParams(vmem_limit_bytes=LIMIT)
    vmem, smem = whole(pltpu.VMEM), whole(pltpu.SMEM)
    near = lambda array: pltpu.with_memory_space_constraint(array, pltpu.VMEM)
    blank = pl.pallas_call(
        first_kernel,
        out_shape=pltpu.VMEM((CODE_ROWS, cols), jnp.float32),
        in_specs=[],
        out_specs=vmem,
        compiler_params=params,
        cost_estimate=pl.CostEstimate(flops=8 * 10**9, bytes_accessed=2**24, transcendentals=0),
        name="first",
    )()
    pick = pltpu.VMEM((2 * rows, rows), jnp.bfloat16)
    message, late, lower, upper = pl.pallas_call(
        product_kernel,
        out_shape=(
            pltpu.VMEM((rows + block + CODE_ROWS, cols), jnp.bfloat16),
            pltpu.VMEM((block, cols), jnp.bfloat16),
            pick,
            pick,
        ),
        in_specs=[vmem] * 7 + [smem, smem],
        out_specs=(vmem,) * 4,
        compiler_params=params,
        name="product",
    )(near(blank), fronts, omega, own_one, own_two, leaf_map, parent_map, leaf_sizes, parent_count)
    both = lax.all_gather(message, "core")
    pieces = pl.pallas_call(
        place_kernel,
        out_shape=pltpu.VMEM((2 * n_row, 2 * block, cols), jnp.bfloat16),
        in_specs=[vmem] * 4,
        out_specs=vmem,
        compiler_params=params,
        name="place",
    )(near(message), near(both), near(lower), near(upper))
    pieces = lax.all_to_all(pieces, ("row", "y"), 0, 0)
    shape = jax.ShapeDtypeStruct(own_one.shape, jnp.bfloat16)
    return pl.pallas_call(
        sum_kernel,
        out_shape=(shape, shape),
        in_specs=[vmem, vmem, vmem],
        out_specs=(vmem, vmem),
        compiler_params=params,
        name="total",
    )(near(pieces), near(message), near(late))


def solution(mesh):
    n_cube, n_row = mesh.devices.shape
    grouped = Mesh(mesh.devices.reshape(n_cube // 4, 2, 2, n_row), ("group", "y", "core", "row"))
    cube = ("group", "y", "core")
    in_specs = (
        P(cube, None, "row"),
        P(cube, "row", None),
        P(cube),
        P(cube, None),
        P(cube, "row", None),
        P(cube),
        P(cube, None),
        P(cube, "row", None),
    )
    out_specs = (P(cube, "row", None), P(cube, "row", None))
    return jax.shard_map(body, mesh=grouped, in_specs=in_specs, out_specs=out_specs, check_vma=False)
```

time: 27.6 us -> 25.7 us (0.931)
  starting transfers between devices: 8.79 us -> 0 us
  blocking collectives: 12.6 us -> 20.3 us
  waiting for transfers between devices: 0.78 us -> 0 us
    ppermute x1 -> x0, starting transfers between devices: 8.79 us -> none  [body(): sibling = lax.ppermute(message, 'core', [(0, 1), (1, 0)])]
    all_gather x0 -> x1, blocking collectives: none -> 8.57 us  [body(): both = lax.all_gather(message, 'core')]
    all_to_all x1, blocking collectives: 12.6 us -> 11.8 us  [body(): pieces = lax.all_to_all(pieces, ('row', 'y'), 0, 0)]
    ppermute x1 -> x0, waiting for transfers between devices: 0.78 us -> none  [body(): sibling = lax.ppermute(message, 'core', [(0, 1), (1, 0)])]
  transfers between devices with their start and end apart: 1 -> 0, of which waited for: 1 -> 0; matrix products, arithmetic and copies ran while one was open for 0% -> 0% of each run, Pallas kernels for 1% -> 0%
where the time goes in v3:
time: 25.7 us; the launch traced here: 25.6 us
  blocking collectives  20.3 us (79%)
  between operations  2.63 us (10%)
  Pallas kernels  2.3 us (9%)
  local copies, waits for them, and re-layouts  0.34 us (1%)
    all_to_all x1, blocking collectives, body(): pieces = lax.all_to_all(pieces, ('row', 'y'), 0, 0)  11.8 us
    all_gather x1, blocking collectives, body(): both = lax.all_gather(message, 'core')  8.57 us
    pallas_call x1, Pallas kernels, body(): pl.pallas_call(product_kernel, out_shape=(pltpu.VMEM((rows + block + CODE...  0.81 us
    pallas_call x1, Pallas kernels, body(): pl.pallas_call(place_kernel, out_shape=pltpu.VMEM((2 * n_row, 2 * block,...  0.81 us
    pallas_call x1, Pallas kernels, body(): pl.pallas_call(sum_kernel, out_shape=(shape, shape), in_specs=[vmem, vmem...  0.68 us

profile of v3, /device:TPU:1, one launch (start us, length us, event | category | flops | bytes accessed | tf_op | source)
XLA Modules:
  0.0 25.6 jit_solution(3681648681696660202)
XLA Ops:
  0.6 0.0 copy-start.3
  0.6 0.0 copy-start.5
  0.7 0.0 copy-start.2
  0.7 0.0 copy-start.4
  0.7 0.0 copy-start.1
  0.7 0.0 copy-start
  2.6 0.0 copy-done.3
  2.6 0.0 copy-done.5
  2.6 0.0 copy-done.2
  2.6 0.0 copy-done.4
  2.6 0.0 copy-done.1
  2.6 0.3 %copy-done = bf16[1,256,4096]{2,1,0:T(8,128)(2,1)S(1)} copy-done((bf16[1,256,4096]{2,1,0:T(8,128)(2,1)S(1)}, bf16[1,256,4096]{2,1,0:T(8,128)(2,1)}, u32[]{:S(2)}) %copy-start) | copy-done | bytes 2097176
  3.0 0.8 %product.1 = (bf16[336,256]{1,0:T(8,128)(2,1)S(1)}, bf16[64,256]{1,0:T(8,128)(2,1)S(1)}, bf16[512,256]{1,0:T(8,128)(2,1)S(1)}, bf16[512,256]{1,0:T(8,128)(2,1)S(1)}) custom-call(f32[16,256]{1,0:T(8,128)S(1)} %first.1.blank, bf16[1,256,4096]{2,1,0:T(8,128)(2,1)S(1)} %copy-done, bf16[1,4096,256]{2,1,0:T(8,128)(2,1)S(1)} %copy-done.1, ...), custom_call_target="tpu_custom_call" | custom-call | tf_op jit(solution)/shard_map/product/pallas_call | solution.py:110
  3.8 8.6 %all-gather = bf16[672,256]{1,0:T(8,128)(2,1)S(1)} all-gather(bf16[336,256]{1,0:T(8,128)(2,1)S(1)} %get-tuple-element.6.mine.message), channel_id=2, replica_groups=mesh['group'=32,'y'=2,'core'=2,'row'=4] {'core'}, dimensions={0}, use_global_device_ids=true | all-gather | bytes 516096 | tf_op jit(solution)/shard_map/all_gather | solution.py:123
  12.3 0.8 %place.1 = bf16[8,128,256]{2,1,0:T(8,128)(2,1)S(1)} custom-call(bf16[336,256]{1,0:T(8,128)(2,1)S(1)} %get-tuple-element.6.mine.message, bf16[2,336,256]{2,1,0:T(8,128)(2,1)S(1)} %bitcast.1, bf16[512,256]{1,0:T(8,128)(2,1)S(1)} %get-tuple-element.7.lower, bf16[512,256]{1,0:T(8,128)(2,1)S(1)} %get-tuple-element.8.upper), custom_call_target="tpu_custom_call" | custom-call | tf_op jit(solution)/shard_map/place/pallas_call | solution.py:124
  13.2 11.8 %all_to_all.5.pieces = bf16[8,128,256]{2,1,0:T(8,128)(2,1)S(1)} all-to-all(bf16[8,128,256]{2,1,0:T(8,128)(2,1)S(1)} %place.1), channel_id=1, replica_groups=mesh['group'=32,'y'=2,'core'=2,'row'=4] {'row','y'}, dimensions={0} | all-to-all | bytes 1048576 | tf_op jit(solution)/shard_map/all_to_all | solution.py:132
  24.9 0.7 %total.1 = (bf16[1,64,256]{2,1,0:T(8,128)(2,1)}, bf16[1,64,256]{2,1,0:T(8,128)(2,1)}) custom-call(bf16[8,128,256]{2,1,0:T(8,128)(2,1)S(1)} %all_to_all.5.pieces, bf16[336,256]{1,0:T(8,128)(2,1)S(1)} %get-tuple-element.6.mine.message, bf16[64,256]{1,0:T(8,128)(2,1)S(1)} %get-tuple-element.9.own_two), custom_call_target="tpu_custom_call" | custom-call | tf_op jit(solution)/shard_map/total/pallas_call | solution.py:134
  (1 shorter events, 0.0 us)
Async XLA Ops:
  0.6 2.0 %copy-start.3 = (bf16[1,64,256]{2,1,0:T(8,128)(2,1)S(1)}, bf16[1,64,256]{2,1,0:T(8,128)(2,1)}, u32[]{:S(2)}) copy-start(bf16[1,64,256]{2,1,0:T(8,128)(2,1)} %own_two.1) | copy-start | bytes 98308
  0.6 2.0 %copy-start.5 = (s32[1,256]{1,0:T(1,128)S(1)}, s32[1,256]{1,0:T(1,128)}, u32[]{:S(2)}) copy-start(s32[1,256]{1,0:T(1,128)} %parent_map.1) | copy-start | bytes 3076
  0.7 2.0 %copy-start.2 = (bf16[1,64,256]{2,1,0:T(8,128)(2,1)S(1)}, bf16[1,64,256]{2,1,0:T(8,128)(2,1)}, u32[]{:S(2)}) copy-start(bf16[1,64,256]{2,1,0:T(8,128)(2,1)} %own_one.1) | copy-start | bytes 98308
  0.7 2.0 %copy-start.4 = (s32[1,256]{1,0:T(1,128)S(1)}, s32[1,256]{1,0:T(1,128)}, u32[]{:S(2)}) copy-start(s32[1,256]{1,0:T(1,128)} %leaf_map.1) | copy-start | bytes 3076
  0.7 2.0 %copy-start.1 = (bf16[1,4096,256]{2,1,0:T(8,128)(2,1)S(1)}, bf16[1,4096,256]{2,1,0:T(8,128)(2,1)}, u32[]{:S(2)}) copy-start(bf16[1,4096,256]{2,1,0:T(8,128)(2,1)} %omega.1) | copy-start | bytes 6291460
  0.7 2.3 %copy-start = (bf16[1,256,4096]{2,1,0:T(8,128)(2,1)S(1)}, bf16[1,256,4096]{2,1,0:T(8,128)(2,1)}, u32[]{:S(2)}) copy-start(bf16[1,256,4096]{2,1,0:T(8,128)(2,1)} %fronts.1) | copy-start | bytes 6291460

commit v4 on v3

--- a/solution.py
+++ b/solution.py
@@ -24,21 +24,26 @@
     out[...] = jnp.zeros_like(out)
 
 
-def product_kernel(blank, fronts, omega, own_one, own_two, leaf_map, parent_map, leaf_size, count, out, two, lower, upper):
-    rows = fronts.shape[1]
-    mine = own_one.shape[1]
+def index_kernel(blank, leaf_map, parent_map, leaf_size, count, code, lower, upper):
+    rows = leaf_map.shape[1]
     core = lax.axis_index("core")
     place = lax.broadcasted_iota(jnp.int32, (1, rows), 1)
     leaf = jnp.where(place < leaf_size[0], leaf_map[...], -1)
     parent = jnp.where(place < count[0], parent_map[...], -1)
     line = lax.broadcasted_iota(jnp.int32, (CODE_ROWS, rows), 0)
-    code = jnp.where(line < 2, leaf, parent)
-    code = jnp.where(line % 2 == 0, code >> 5, code & (DIGIT - 1))
-    out[rows + mine :, :] = (code.astype(jnp.float32) + blank[...]).astype(jnp.bfloat16)
-    out[rows : rows + mine, :] = own_one[0]
-    two[...] = own_two[0]
+    digits = jnp.where(line < 2, leaf, parent)
+    digits = jnp.where(line % 2 == 0, digits >> 5, digits & (DIGIT - 1))
+    code[...] = (digits.astype(jnp.float32) + blank[...]).astype(jnp.bfloat16)
     lower[...] = picks((core, 1 - core), leaf)
     upper[...] = picks((core, core + 2), parent)
+
+
+def product_kernel(fronts, omega, own_one, own_two, code, out, two):
+    rows = fronts.shape[1]
+    mine = own_one.shape[1]
+    out[rows : rows + mine, :] = own_one[0]
+    out[rows + mine :, :] = code[...]
+    two[...] = own_two[0]
     out[:rows, :] = jnp.dot(fronts[0], omega[0], preferred_element_type=jnp.float32).astype(jnp.bfloat16)
 
 
@@ -53,26 +58,31 @@
     rows = out.shape[2]
     block = out.shape[1] // 2
     n_row = rows // block
-    core, row = lax.axis_index("core"), lax.axis_index("row")
+    core, row, here = lax.axis_index("core"), lax.axis_index("row"), lax.axis_index("y")
     other = both.at[1 - core]
     leaf, parent = decode(other[rows + block :, :])
-    parents = jnp.dot(lower[...], mine[:rows, :], preferred_element_type=jnp.float32)
-    parents += jnp.dot(picks((core, 1 - core), leaf), other[:rows, :], preferred_element_type=jnp.float32)
-    level_one = parents[:rows].astype(jnp.bfloat16)
+    other_lower, other_upper = picks((core, 1 - core), leaf), picks((core, core + 2), parent)
+    partial = jnp.concatenate([mine[:rows, :], other[:rows, :]], axis=0)
+    line = lax.broadcasted_iota(jnp.int32, (rows, 1), 0) // block == row
+    halves = []
+    for k, source in enumerate((mine, other)):
+        part = slice(k * rows, (k + 1) * rows)
+        pick = jnp.concatenate([lower[part], other_lower[part]], axis=1)
+        half = jnp.dot(pick, partial, preferred_element_type=jnp.float32)
+        if k == 0:
+            level_one = half.astype(jnp.bfloat16)
+        own = jnp.concatenate([source[rows : rows + block, :]] * n_row, axis=0)
+        halves.append(jnp.where(line, half + own.astype(jnp.float32), half).astype(jnp.bfloat16))
+    parents = jnp.concatenate(halves, axis=0)
     for x in range(n_row):
-        for y in range(2):
-            out[2 * x + y, block:, :] = level_one[x * block : (x + 1) * block]
-    line = lax.broadcasted_iota(jnp.int32, (rows, 1), 0) // block == row
-    own = jnp.concatenate([mine[rows : rows + block, :]] * n_row, axis=0).astype(jnp.float32)
-    half = (parents[:rows] + jnp.where(line, own, 0.0)).astype(jnp.bfloat16)
-    placed = jnp.dot(upper[...], half, preferred_element_type=jnp.float32)
-    own = jnp.concatenate([other[rows : rows + block, :]] * n_row, axis=0).astype(jnp.float32)
-    half = (parents[rows:] + jnp.where(line, own, 0.0)).astype(jnp.bfloat16)
-    placed += jnp.dot(picks((core, core + 2), parent), half, preferred_element_type=jnp.float32)
-    placed = placed.astype(jnp.bfloat16)
-    for x in range(n_row):
-        for y in range(2):
-            out[2 * x + y, :block, :] = placed[y * rows + x * block : y * rows + (x + 1) * block]
+        out[2 * x + here, block:, :] = level_one[x * block : (x + 1) * block]
+        out[2 * x + 1 - here, block:, :] = jnp.zeros((block, rows), jnp.bfloat16)
+    for y in range(2):
+        part = slice(y * rows, (y + 1) * rows)
+        pick = jnp.concatenate([upper[part], other_upper[part]], axis=1)
+        placed = jnp.dot(pick, parents, preferred_element_type=jnp.float32).astype(jnp.bfloat16)
+        for x in range(n_row):
+            out[2 * x + y, :block, :] = placed[x * block : (x + 1) * block]
 
 
 def sum_kernel(pieces, message, own_two, one, two):
@@ -107,19 +117,25 @@
         name="first",
     )()
     pick = pltpu.VMEM((2 * rows, rows), jnp.bfloat16)
-    message, late, lower, upper = pl.pallas_call(
+    code, lower, upper = pl.pallas_call(
+        index_kernel,
+        out_shape=(pltpu.VMEM((CODE_ROWS, rows), jnp.bfloat16), pick, pick),
+        in_specs=[vmem] * 3 + [smem, smem],
+        out_specs=(vmem,) * 3,
+        compiler_params=params,
+        name="index",
+    )(near(blank), leaf_map, parent_map, leaf_sizes, parent_count)
+    message, late = pl.pallas_call(
         product_kernel,
         out_shape=(
             pltpu.VMEM((rows + block + CODE_ROWS, cols), jnp.bfloat16),
             pltpu.VMEM((block, cols), jnp.bfloat16),
-            pick,
-            pick,
         ),
-        in_specs=[vmem] * 7 + [smem, smem],
-        out_specs=(vmem,) * 4,
+        in_specs=[vmem] * 5,
+        out_specs=(vmem,) * 2,
         compiler_params=params,
         name="product",
-    )(near(blank), fronts, omega, own_one, own_two, leaf_map, parent_map, leaf_sizes, parent_count)
+    )(fronts, omega, own_one, own_two, near(code))
     both = lax.all_gather(message, "core")
     pieces = pl.pallas_call(
         place_kernel,

time: 25.7 us -> 25.4 us (0.988)
  no operation moved by 1% of the time
where the time goes in v4:
time: 25.4 us; the launch traced here: 25.2 us
  blocking collectives  20.3 us (80%)
  between operations  2.64 us (10%)
  Pallas kernels  2.07 us (8%)
    all_to_all x1, blocking collectives, body(): pieces = lax.all_to_all(pieces, ('row', 'y'), 0, 0)  11.8 us
    all_gather x1, blocking collectives, body(): both = lax.all_gather(message, 'core')  8.56 us
    pallas_call x1, Pallas kernels, body(): pl.pallas_call(product_kernel, out_shape=(pltpu.VMEM((rows + block + CODE...  0.71 us
    pallas_call x1, Pallas kernels, body(): pl.pallas_call(sum_kernel, out_shape=(shape, shape), in_specs=[vmem, vmem...  0.68 us
    pallas_call x1, Pallas kernels, body(): pl.pallas_call(place_kernel, out_shape=pltpu.VMEM((2 * n_row, 2 * block,...  0.57 us

profile of v4, /device:TPU:1, one launch (start us, length us, event | category | flops | bytes accessed | tf_op | source)
XLA Modules:
  0.0 25.2 jit_solution(10859944148535152282)
XLA Ops:
  0.6 0.0 copy-start.5
  0.6 0.0 copy-start.4
  0.7 0.0 copy-start.3
  0.7 0.0 copy-start.2
  0.7 0.0 copy-start.1
  0.7 0.0 copy-start
  2.6 0.0 copy-done.5
  2.6 0.0 copy-done.4
  2.6 0.1 index.1
  2.7 0.0 copy-done.3
  2.7 0.0 copy-done.2
  2.8 0.0 copy-done.1
  2.8 0.2 copy-done
  3.0 0.7 %product.1 = (bf16[336,256]{1,0:T(8,128)(2,1)S(1)}, bf16[64,256]{1,0:T(8,128)(2,1)S(1)}) custom-call(bf16[1,256,4096]{2,1,0:T(8,128)(2,1)S(1)} %copy-done, bf16[1,4096,256]{2,1,0:T(8,128)(2,1)S(1)} %copy-done.1, bf16[1,64,256]{2,1,0:T(8,128)(2,1)S(1)} %copy-done.2, bf16[1,64,256]{2,1,0:T(8,128)(2,1)S(1)} %copy-done.3, bf16[16,256]{1,0:T(8,128)(2,1)S(1)} %get-tuple-element.7.code), custom_call_target="tpu_custom_call" | custom-call | tf_op jit(solution)/shard_map/product/pallas_call | solution.py:128
  3.7 8.6 %all-gather = bf16[672,256]{1,0:T(8,128)(2,1)S(1)} all-gather(bf16[336,256]{1,0:T(8,128)(2,1)S(1)} %get-tuple-element.8.mine.message), channel_id=2, replica_groups=mesh['group'=32,'y'=2,'core'=2,'row'=4] {'core'}, dimensions={0}, use_global_device_ids=true | all-gather | bytes 516096 | tf_op jit(solution)/shard_map/all_gather | solution.py:139
  12.2 0.6 %place.1 = bf16[8,128,256]{2,1,0:T(8,128)(2,1)S(1)} custom-call(bf16[336,256]{1,0:T(8,128)(2,1)S(1)} %get-tuple-element.8.mine.message, bf16[2,336,256]{2,1,0:T(8,128)(2,1)S(1)} %bitcast.1, bf16[512,256]{1,0:T(8,128)(2,1)S(1)} %get-tuple-element.9.lower, bf16[512,256]{1,0:T(8,128)(2,1)S(1)} %get-tuple-element.10.upper), custom_call_target="tpu_custom_call" | custom-call | tf_op jit(solution)/shard_map/place/pallas_call | solution.py:140
  12.8 11.8 %all_to_all.5.pieces = bf16[8,128,256]{2,1,0:T(8,128)(2,1)S(1)} all-to-all(bf16[8,128,256]{2,1,0:T(8,128)(2,1)S(1)} %place.1), channel_id=1, replica_groups=mesh['group'=32,'y'=2,'core'=2,'row'=4] {'row','y'}, dimensions={0} | all-to-all | bytes 1048576 | tf_op jit(solution)/shard_map/all_to_all | solution.py:148
  24.6 0.7 %total.1 = (bf16[1,64,256]{2,1,0:T(8,128)(2,1)}, bf16[1,64,256]{2,1,0:T(8,128)(2,1)}) custom-call(bf16[8,128,256]{2,1,0:T(8,128)(2,1)S(1)} %all_to_all.5.pieces, bf16[336,256]{1,0:T(8,128)(2,1)S(1)} %get-tuple-element.8.mine.message, bf16[64,256]{1,0:T(8,128)(2,1)S(1)} %get-tuple-element.11.own_two), custom_call_target="tpu_custom_call" | custom-call | tf_op jit(solution)/shard_map/total/pallas_call | solution.py:150
  (1 shorter events, 0.0 us)
Async XLA Ops:
  0.6 2.0 %copy-start.5 = (s32[1,256]{1,0:T(1,128)S(1)}, s32[1,256]{1,0:T(1,128)}, u32[]{:S(2)}) copy-start(s32[1,256]{1,0:T(1,128)} %parent_map.1) | copy-start | bytes 3076
  0.6 2.0 %copy-start.4 = (s32[1,256]{1,0:T(1,128)S(1)}, s32[1,256]{1,0:T(1,128)}, u32[]{:S(2)}) copy-start(s32[1,256]{1,0:T(1,128)} %leaf_map.1) | copy-start | bytes 3076
  0.7 2.1 %copy-start.3 = (bf16[1,64,256]{2,1,0:T(8,128)(2,1)S(1)}, bf16[1,64,256]{2,1,0:T(8,128)(2,1)}, u32[]{:S(2)}) copy-start(bf16[1,64,256]{2,1,0:T(8,128)(2,1)} %own_two.1) | copy-start | bytes 98308
  0.7 2.1 %copy-start.2 = (bf16[1,64,256]{2,1,0:T(8,128)(2,1)S(1)}, bf16[1,64,256]{2,1,0:T(8,128)(2,1)}, u32[]{:S(2)}) copy-start(bf16[1,64,256]{2,1,0:T(8,128)(2,1)} %own_one.1) | copy-start | bytes 98308
  0.7 2.1 %copy-start.1 = (bf16[1,4096,256]{2,1,0:T(8,128)(2,1)S(1)}, bf16[1,4096,256]{2,1,0:T(8,128)(2,1)}, u32[]{:S(2)}) copy-start(bf16[1,4096,256]{2,1,0:T(8,128)(2,1)} %omega.1) | copy-start | bytes 6291460
  0.7 2.3 %copy-start = (bf16[1,256,4096]{2,1,0:T(8,128)(2,1)S(1)}, bf16[1,256,4096]{2,1,0:T(8,128)(2,1)}, u32[]{:S(2)}) copy-start(bf16[1,256,4096]{2,1,0:T(8,128)(2,1)} %fronts.1) | copy-start | bytes 6291460

commit v5 on v4

--- a/solution.py
+++ b/solution.py
@@ -35,16 +35,20 @@
     digits = jnp.where(line % 2 == 0, digits >> 5, digits & (DIGIT - 1))
     code[...] = (digits.astype(jnp.float32) + blank[...]).astype(jnp.bfloat16)
     lower[...] = picks((core, 1 - core), leaf)
-    upper[...] = picks((core, core + 2), parent)
+    here = lax.axis_index("y")
+    upper[...] = picks((core + 2 * here, core + 2 - 2 * here), parent)
 
 
-def product_kernel(fronts, omega, own_one, own_two, code, out, two):
+def product_kernel(fronts, omega, own_one, own_two, code, out, rest, two):
     rows = fronts.shape[1]
     mine = own_one.shape[1]
     out[rows : rows + mine, :] = own_one[0]
     out[rows + mine :, :] = code[...]
     two[...] = own_two[0]
-    out[:rows, :] = jnp.dot(fronts[0], omega[0], preferred_element_type=jnp.float32).astype(jnp.bfloat16)
+    partial = jnp.dot(fronts[0], omega[0], preferred_element_type=jnp.float32)
+    high = partial.astype(jnp.bfloat16)
+    out[:rows, :] = high
+    rest[...] = (partial - high.astype(jnp.float32)).astype(jnp.bfloat16)
 
 
 def decode(code):
@@ -54,35 +58,41 @@
     return leaf.astype(jnp.int32), parent.astype(jnp.int32)
 
 
-def place_kernel(mine, both, lower, upper, out):
+def place_kernel(mine, rest, both, lower, upper, out):
     rows = out.shape[2]
     block = out.shape[1] // 2
     n_row = rows // block
     core, row, here = lax.axis_index("core"), lax.axis_index("row"), lax.axis_index("y")
     other = both.at[1 - core]
     leaf, parent = decode(other[rows + block :, :])
-    other_lower, other_upper = picks((core, 1 - core), leaf), picks((core, core + 2), parent)
-    partial = jnp.concatenate([mine[:rows, :], other[:rows, :]], axis=0)
+    other_lower = picks((core, 1 - core), leaf)
+    other_upper = picks((core + 2 * here, core + 2 - 2 * here), parent)
+    partial = jnp.concatenate([mine[:rows, :], rest[...], other[:rows, :]], axis=0)
     line = lax.broadcasted_iota(jnp.int32, (rows, 1), 0) // block == row
-    halves = []
+    highs, lows = [], []
     for k, source in enumerate((mine, other)):
         part = slice(k * rows, (k + 1) * rows)
-        pick = jnp.concatenate([lower[part], other_lower[part]], axis=1)
+        pick = jnp.concatenate([lower[part], lower[part], other_lower[part]], axis=1)
         half = jnp.dot(pick, partial, preferred_element_type=jnp.float32)
         if k == 0:
             level_one = half.astype(jnp.bfloat16)
         own = jnp.concatenate([source[rows : rows + block, :]] * n_row, axis=0)
-        halves.append(jnp.where(line, half + own.astype(jnp.float32), half).astype(jnp.bfloat16))
-    parents = jnp.concatenate(halves, axis=0)
+        half = jnp.where(line, half + own.astype(jnp.float32), half)
+        highs.append(half.astype(jnp.bfloat16))
+        lows.append((half - highs[k].astype(jnp.float32)).astype(jnp.bfloat16))
     for x in range(n_row):
         out[2 * x + here, block:, :] = level_one[x * block : (x + 1) * block]
-        out[2 * x + 1 - here, block:, :] = jnp.zeros((block, rows), jnp.bfloat16)
-    for y in range(2):
-        part = slice(y * rows, (y + 1) * rows)
+    high, low = jnp.concatenate(highs, axis=0), jnp.concatenate(lows, axis=0)
+    for k, y in enumerate((here, 1 - here)):
+        part = slice(k * rows, (k + 1) * rows)
         pick = jnp.concatenate([upper[part], other_upper[part]], axis=1)
-        placed = jnp.dot(pick, parents, preferred_element_type=jnp.float32).astype(jnp.bfloat16)
+        placed = jnp.dot(pick, high, preferred_element_type=jnp.float32).astype(jnp.bfloat16)
         for x in range(n_row):
             out[2 * x + y, :block, :] = placed[x * block : (x + 1) * block]
+        if k == 1:
+            placed = jnp.dot(pick, low, preferred_element_type=jnp.float32).astype(jnp.bfloat16)
+            for x in range(n_row):
+                out[2 * x + y, block:, :] = placed[x * block : (x + 1) * block]
 
 
 def sum_kernel(pieces, message, own_two, one, two):
@@ -96,6 +106,8 @@
     total = own_two[...].astype(jnp.float32)
     for k in range(2 * n_row):
         total += pieces[k, :block, :].astype(jnp.float32)
+    for x in range(n_row):
+        total += pieces[2 * x + 1 - y, block:, :].astype(jnp.float32)
     two[0] = total.astype(jnp.bfloat16)
 
 
@@ -125,14 +137,15 @@
         compiler_params=params,
         name="index",
     )(near(blank), leaf_map, parent_map, leaf_sizes, parent_count)
-    message, late = pl.pallas_call(
+    message, rest, late = pl.pallas_call(
         product_kernel,
         out_shape=(
             pltpu.VMEM((rows + block + CODE_ROWS, cols), jnp.bfloat16),
+            pltpu.VMEM((rows, cols), jnp.bfloat16),
             pltpu.VMEM((block, cols), jnp.bfloat16),
         ),
         in_specs=[vmem] * 5,
-        out_specs=(vmem,) * 2,
+        out_specs=(vmem,) * 3,
         compiler_params=params,
         name="product",
     )(fronts, omega, own_one, own_two, near(code))
@@ -140,11 +153,11 @@
     pieces = pl.pallas_call(
         place_kernel,
         out_shape=pltpu.VMEM((2 * n_row, 2 * block, cols), jnp.bfloat16),
-        in_specs=[vmem] * 4,
+        in_specs=[vmem] * 5,
         out_specs=vmem,
         compiler_params=params,
         name="place",
-    )(near(message), near(both), near(lower), near(upper))
+    )(near(message), near(rest), near(both), near(lower), near(upper))
     pieces = lax.all_to_all(pieces, ("row", "y"), 0, 0)
     shape = jax.ShapeDtypeStruct(own_one.shape, jnp.bfloat16)
     return pl.pallas_call(

time: 25.4 us -> 25.7 us (1.012)
  no operation moved by 1% of the time
where the time goes in v5:
time: 25.7 us; the launch traced here: 25.5 us
  blocking collectives  20.3 us (79%)
  between operations  2.64 us (10%)
  Pallas kernels  2.31 us (9%)
    all_to_all x1, blocking collectives, body(): pieces = lax.all_to_all(pieces, ('row', 'y'), 0, 0)  11.8 us
    all_gather x1, blocking collectives, body(): both = lax.all_gather(message, 'core')  8.56 us
    pallas_call x1, Pallas kernels, body(): pl.pallas_call(place_kernel, out_shape=pltpu.VMEM((2 * n_row, 2 * block,...  0.78 us
    pallas_call x1, Pallas kernels, body(): pl.pallas_call(product_kernel, out_shape=(pltpu.VMEM((rows + block + CODE...  0.71 us
    pallas_call x1, Pallas kernels, body(): pl.pallas_call(sum_kernel, out_shape=(shape, shape), in_specs=[vmem, vmem...  0.7 us

profile of v5, /device:TPU:1, one launch (start us, length us, event | category | flops | bytes accessed | tf_op | source)
XLA Modules:
  0.0 25.5 jit_solution(18158190168849815493)
XLA Ops:
  0.6 0.0 copy-start.5
  0.6 0.0 copy-start.4
  0.7 0.0 copy-start.3
  0.7 0.0 copy-start.2
  0.7 0.0 copy-start.1
  0.7 0.0 copy-start
  2.6 0.0 copy-done.5
  2.6 0.0 copy-done.4
  2.6 0.1 index.1
  2.7 0.0 copy-done.3
  2.7 0.0 copy-done.2
  2.8 0.0 copy-done.1
  2.8 0.2 copy-done
  3.0 0.7 %product.1 = (bf16[336,256]{1,0:T(8,128)(2,1)S(1)}, bf16[256,256]{1,0:T(8,128)(2,1)S(1)}, bf16[64,256]{1,0:T(8,128)(2,1)S(1)}) custom-call(bf16[1,256,4096]{2,1,0:T(8,128)(2,1)S(1)} %copy-done, bf16[1,4096,256]{2,1,0:T(8,128)(2,1)S(1)} %copy-done.1, bf16[1,64,256]{2,1,0:T(8,128)(2,1)S(1)} %copy-done.2, bf16[1,64,256]{2,1,0:T(8,128)(2,1)S(1)} %copy-done.3, ...), custom_call_target="tpu_custom_call" | custom-call | tf_op jit(solution)/shard_map/product/pallas_call | solution.py:140
  3.7 8.6 %all-gather = bf16[672,256]{1,0:T(8,128)(2,1)S(1)} all-gather(bf16[336,256]{1,0:T(8,128)(2,1)S(1)} %get-tuple-element.9.mine.message), channel_id=2, replica_groups=mesh['group'=32,'y'=2,'core'=2,'row'=4] {'core'}, dimensions={0}, use_global_device_ids=true | all-gather | bytes 516096 | tf_op jit(solution)/shard_map/all_gather | solution.py:152
  12.2 0.8 %place.1 = bf16[8,128,256]{2,1,0:T(8,128)(2,1)S(1)} custom-call(bf16[336,256]{1,0:T(8,128)(2,1)S(1)} %get-tuple-element.9.mine.message, bf16[256,256]{1,0:T(8,128)(2,1)S(1)} %get-tuple-element.10.rest, bf16[2,336,256]{2,1,0:T(8,128)(2,1)S(1)} %bitcast.1, bf16[512,256]{1,0:T(8,128)(2,1)S(1)} %get-tuple-element.11.lower, ...), custom_call_target="tpu_custom_call" | custom-call | tf_op jit(solution)/shard_map/place/pallas_call | solution.py:153
  13.0 11.8 %all_to_all.5.pieces = bf16[8,128,256]{2,1,0:T(8,128)(2,1)S(1)} all-to-all(bf16[8,128,256]{2,1,0:T(8,128)(2,1)S(1)} %place.1), channel_id=1, replica_groups=mesh['group'=32,'y'=2,'core'=2,'row'=4] {'row','y'}, dimensions={0} | all-to-all | bytes 1048576 | tf_op jit(solution)/shard_map/all_to_all | solution.py:161
  24.8 0.7 %total.1 = (bf16[1,64,256]{2,1,0:T(8,128)(2,1)}, bf16[1,64,256]{2,1,0:T(8,128)(2,1)}) custom-call(bf16[8,128,256]{2,1,0:T(8,128)(2,1)S(1)} %all_to_all.5.pieces, bf16[336,256]{1,0:T(8,128)(2,1)S(1)} %get-tuple-element.9.mine.message, bf16[64,256]{1,0:T(8,128)(2,1)S(1)} %get-tuple-element.13.own_two), custom_call_target="tpu_custom_call" | custom-call | tf_op jit(solution)/shard_map/total/pallas_call | solution.py:163
  (1 shorter events, 0.0 us)
Async XLA Ops:
  0.6 2.0 %copy-start.5 = (s32[1,256]{1,0:T(1,128)S(1)}, s32[1,256]{1,0:T(1,128)}, u32[]{:S(2)}) copy-start(s32[1,256]{1,0:T(1,128)} %parent_map.1) | copy-start | bytes 3076
  0.6 2.0 %copy-start.4 = (s32[1,256]{1,0:T(1,128)S(1)}, s32[1,256]{1,0:T(1,128)}, u32[]{:S(2)}) copy-start(s32[1,256]{1,0:T(1,128)} %leaf_map.1) | copy-start | bytes 3076
  0.7 2.1 %copy-start.3 = (bf16[1,64,256]{2,1,0:T(8,128)(2,1)S(1)}, bf16[1,64,256]{2,1,0:T(8,128)(2,1)}, u32[]{:S(2)}) copy-start(bf16[1,64,256]{2,1,0:T(8,128)(2,1)} %own_two.1) | copy-start | bytes 98308
  0.7 2.1 %copy-start.2 = (bf16[1,64,256]{2,1,0:T(8,128)(2,1)S(1)}, bf16[1,64,256]{2,1,0:T(8,128)(2,1)}, u32[]{:S(2)}) copy-start(bf16[1,64,256]{2,1,0:T(8,128)(2,1)} %own_one.1) | copy-start | bytes 98308
  0.7 2.1 %copy-start.1 = (bf16[1,4096,256]{2,1,0:T(8,128)(2,1)S(1)}, bf16[1,4096,256]{2,1,0:T(8,128)(2,1)}, u32[]{:S(2)}) copy-start(bf16[1,4096,256]{2,1,0:T(8,128)(2,1)} %omega.1) | copy-start | bytes 6291460
  0.7 2.3 %copy-start = (bf16[1,256,4096]{2,1,0:T(8,128)(2,1)S(1)}, bf16[1,256,4096]{2,1,0:T(8,128)(2,1)}, u32[]{:S(2)}) copy-start(bf16[1,256,4096]{2,1,0:T(8,128)(2,1)} %fronts.1) | copy-start | bytes 6291460

commit v6 on v5

--- a/solution.py
+++ b/solution.py
@@ -24,7 +24,7 @@
     out[...] = jnp.zeros_like(out)
 
 
-def index_kernel(blank, leaf_map, parent_map, leaf_size, count, code, lower, upper):
+def index_kernel(blank, leaf_map, parent_map, leaf_size, count, code, lower):
     rows = leaf_map.shape[1]
     core = lax.axis_index("core")
     place = lax.broadcasted_iota(jnp.int32, (1, rows), 1)
@@ -35,8 +35,6 @@
     digits = jnp.where(line % 2 == 0, digits >> 5, digits & (DIGIT - 1))
     code[...] = (digits.astype(jnp.float32) + blank[...]).astype(jnp.bfloat16)
     lower[...] = picks((core, 1 - core), leaf)
-    here = lax.axis_index("y")
-    upper[...] = picks((core + 2 * here, core + 2 - 2 * here), parent)
 
 
 def product_kernel(fronts, omega, own_one, own_two, code, out, rest, two):
@@ -58,41 +56,44 @@
     return leaf.astype(jnp.int32), parent.astype(jnp.int32)
 
 
-def place_kernel(mine, rest, both, lower, upper, out):
+def place_kernel(mine, rest, both, lower, out):
     rows = out.shape[2]
     block = out.shape[1] // 2
     n_row = rows // block
     core, row, here = lax.axis_index("core"), lax.axis_index("row"), lax.axis_index("y")
     other = both.at[1 - core]
-    leaf, parent = decode(other[rows + block :, :])
-    other_lower = picks((core, 1 - core), leaf)
-    other_upper = picks((core + 2 * here, core + 2 - 2 * here), parent)
+    codes = mine[rows + block :, :], other[rows + block :, :]
+    (leaf, parent), (other_leaf, other_parent) = decode(codes[0]), decode(codes[1])
+    other_lower = picks((core, 1 - core), other_leaf)
+    table = jnp.concatenate(codes, axis=1)
+    targets = []
+    for index, pick in ((leaf, lower[...]), (other_leaf, other_lower)):
+        _, target = decode(jnp.dot(table, pick, preferred_element_type=jnp.float32))
+        targets.append(jnp.where(index >= 0, target, -1))
+    own = []
+    for index in (parent, other_parent):
+        turned = pltpu.roll(jnp.broadcast_to(index, (8, rows)), lax.rem(n_row - row, n_row) * block, 1)
+        own.append(turned[:1, :block])
+    own = jnp.concatenate(own, axis=1)
+    line = lax.broadcasted_iota(jnp.int32, (rows, 2 * block), 0)
     partial = jnp.concatenate([mine[:rows, :], rest[...], other[:rows, :]], axis=0)
-    line = lax.broadcasted_iota(jnp.int32, (rows, 1), 0) // block == row
-    highs, lows = [], []
-    for k, source in enumerate((mine, other)):
-        part = slice(k * rows, (k + 1) * rows)
-        pick = jnp.concatenate([lower[part], lower[part], other_lower[part]], axis=1)
-        half = jnp.dot(pick, partial, preferred_element_type=jnp.float32)
-        if k == 0:
-            level_one = half.astype(jnp.bfloat16)
-        own = jnp.concatenate([source[rows : rows + block, :]] * n_row, axis=0)
-        half = jnp.where(line, half + own.astype(jnp.float32), half)
-        highs.append(half.astype(jnp.bfloat16))
-        lows.append((half - highs[k].astype(jnp.float32)).astype(jnp.bfloat16))
+    pick = jnp.concatenate([lower[:rows], lower[:rows], other_lower[:rows]], axis=1)
+    level_one = jnp.dot(pick, partial, preferred_element_type=jnp.float32).astype(jnp.bfloat16)
     for x in range(n_row):
         out[2 * x + here, block:, :] = level_one[x * block : (x + 1) * block]
-    high, low = jnp.concatenate(highs, axis=0), jnp.concatenate(lows, axis=0)
+    partial = jnp.concatenate([partial, mine[rows : rows + block, :], other[rows : rows + block, :]], axis=0)
     for k, y in enumerate((here, 1 - here)):
-        part = slice(k * rows, (k + 1) * rows)
-        pick = jnp.concatenate([upper[part], other_upper[part]], axis=1)
-        placed = jnp.dot(pick, high, preferred_element_type=jnp.float32).astype(jnp.bfloat16)
+        quarter = core + 2 * y
+        picked = picks((quarter,), targets[0])
+        pick = [picked, picked, picks((quarter,), targets[1]), (line + quarter * rows == own).astype(jnp.bfloat16)]
+        placed = jnp.dot(jnp.concatenate(pick, axis=1), partial, preferred_element_type=jnp.float32)
+        high = placed.astype(jnp.bfloat16)
         for x in range(n_row):
-            out[2 * x + y, :block, :] = placed[x * block : (x + 1) * block]
+            out[2 * x + y, :block, :] = high[x * block : (x + 1) * block]
         if k == 1:
-            placed = jnp.dot(pick, low, preferred_element_type=jnp.float32).astype(jnp.bfloat16)
+            low = (placed - high.astype(jnp.float32)).astype(jnp.bfloat16)
             for x in range(n_row):
-                out[2 * x + y, block:, :] = placed[x * block : (x + 1) * block]
+                out[2 * x + y, block:, :] = low[x * block : (x + 1) * block]
 
 
 def sum_kernel(pieces, message, own_two, one, two):
@@ -129,11 +130,11 @@
         name="first",
     )()
     pick = pltpu.VMEM((2 * rows, rows), jnp.bfloat16)
-    code, lower, upper = pl.pallas_call(
+    code, lower = pl.pallas_call(
         index_kernel,
-        out_shape=(pltpu.VMEM((CODE_ROWS, rows), jnp.bfloat16), pick, pick),
+        out_shape=(pltpu.VMEM((CODE_ROWS, rows), jnp.bfloat16), pick),
         in_specs=[vmem] * 3 + [smem, smem],
-        out_specs=(vmem,) * 3,
+        out_specs=(vmem,) * 2,
         compiler_params=params,
         name="index",
     )(near(blank), leaf_map, parent_map, leaf_sizes, parent_count)
@@ -153,11 +154,11 @@
     pieces = pl.pallas_call(
         place_kernel,
         out_shape=pltpu.VMEM((2 * n_row, 2 * block, cols), jnp.bfloat16),
-        in_specs=[vmem] * 5,
+        in_specs=[vmem] * 4,
         out_specs=vmem,
         compiler_params=params,
         name="place",
-    )(near(message), near(rest), near(both), near(lower), near(upper))
+    )(near(message), near(rest), near(both), near(lower))
     pieces = lax.all_to_all(pieces, ("row", "y"), 0, 0)
     shape = jax.ShapeDtypeStruct(own_one.shape, jnp.bfloat16)
     return pl.pallas_call(

time: 25.7 us -> 25.5 us (level)
  no operation moved by 1% of the time
where the time goes in v6:
time: 25.5 us; the launch traced here: 25.3 us
  blocking collectives  20.3 us (80%)
  between operations  2.64 us (10%)
  Pallas kernels  2.08 us (8%)
  local copies, waits for them, and re-layouts  0.26 us (1%)
    all_to_all x1, blocking collectives, body(): pieces = lax.all_to_all(pieces, ('row', 'y'), 0, 0)  11.8 us
    all_gather x1, blocking collectives, body(): both = lax.all_gather(message, 'core')  8.56 us
    pallas_call x1, Pallas kernels, body(): pl.pallas_call(product_kernel, out_shape=(pltpu.VMEM((rows + block + CODE...  0.71 us
    pallas_call x1, Pallas kernels, body(): pl.pallas_call(sum_kernel, out_shape=(shape, shape), in_specs=[vmem, vmem...  0.7 us
    pallas_call x1, Pallas kernels, body(): pl.pallas_call(place_kernel, out_shape=pltpu.VMEM((2 * n_row, 2 * block,...  0.61 us

profile of v6, /device:TPU:1, one launch (start us, length us, event | category | flops | bytes accessed | tf_op | source)
XLA Modules:
  0.0 25.3 jit_solution(11211161156140908719)
XLA Ops:
  0.6 0.0 copy-start.5
  0.6 0.0 copy-start.4
  0.7 0.0 copy-start.3
  0.7 0.0 copy-start.2
  0.7 0.0 copy-start.1
  0.7 0.0 copy-start
  2.6 0.0 copy-done.5
  2.6 0.0 copy-done.4
  2.6 0.1 index.1
  2.7 0.0 copy-done.3
  2.7 0.0 copy-done.2
  2.7 0.0 copy-done.1
  2.7 0.2 copy-done
  3.0 0.7 %product.1 = (bf16[336,256]{1,0:T(8,128)(2,1)S(1)}, bf16[256,256]{1,0:T(8,128)(2,1)S(1)}, bf16[64,256]{1,0:T(8,128)(2,1)S(1)}) custom-call(bf16[1,256,4096]{2,1,0:T(8,128)(2,1)S(1)} %copy-done, bf16[1,4096,256]{2,1,0:T(8,128)(2,1)S(1)} %copy-done.1, bf16[1,64,256]{2,1,0:T(8,128)(2,1)S(1)} %copy-done.2, bf16[1,64,256]{2,1,0:T(8,128)(2,1)S(1)} %copy-done.3, ...), custom_call_target="tpu_custom_call" | custom-call | tf_op jit(solution)/shard_map/product/pallas_call | solution.py:141
  3.7 8.6 %all-gather = bf16[672,256]{1,0:T(8,128)(2,1)S(1)} all-gather(bf16[336,256]{1,0:T(8,128)(2,1)S(1)} %get-tuple-element.8.mine.message), channel_id=2, replica_groups=mesh['group'=32,'y'=2,'core'=2,'row'=4] {'core'}, dimensions={0}, use_global_device_ids=true | all-gather | bytes 516096 | tf_op jit(solution)/shard_map/all_gather | solution.py:153
  12.2 0.6 %place.1 = bf16[8,128,256]{2,1,0:T(8,128)(2,1)S(1)} custom-call(bf16[336,256]{1,0:T(8,128)(2,1)S(1)} %get-tuple-element.8.mine.message, bf16[256,256]{1,0:T(8,128)(2,1)S(1)} %get-tuple-element.9.rest, bf16[2,336,256]{2,1,0:T(8,128)(2,1)S(1)} %bitcast.1, bf16[512,256]{1,0:T(8,128)(2,1)S(1)} %get-tuple-element.10.lower), custom_call_target="tpu_custom_call" | custom-call | tf_op jit(solution)/shard_map/place/pallas_call | solution.py:154
  12.9 11.8 %all_to_all.5.pieces = bf16[8,128,256]{2,1,0:T(8,128)(2,1)S(1)} all-to-all(bf16[8,128,256]{2,1,0:T(8,128)(2,1)S(1)} %place.1), channel_id=1, replica_groups=mesh['group'=32,'y'=2,'core'=2,'row'=4] {'row','y'}, dimensions={0} | all-to-all | bytes 1048576 | tf_op jit(solution)/shard_map/all_to_all | solution.py:162
  24.6 0.7 %total.1 = (bf16[1,64,256]{2,1,0:T(8,128)(2,1)}, bf16[1,64,256]{2,1,0:T(8,128)(2,1)}) custom-call(bf16[8,128,256]{2,1,0:T(8,128)(2,1)S(1)} %all_to_all.5.pieces, bf16[336,256]{1,0:T(8,128)(2,1)S(1)} %get-tuple-element.8.mine.message, bf16[64,256]{1,0:T(8,128)(2,1)S(1)} %get-tuple-element.11.own_two), custom_call_target="tpu_custom_call" | custom-call | tf_op jit(solution)/shard_map/total/pallas_call | solution.py:164
  (1 shorter events, 0.0 us)
Async XLA Ops:
  0.6 2.0 %copy-start.5 = (s32[1,256]{1,0:T(1,128)S(1)}, s32[1,256]{1,0:T(1,128)}, u32[]{:S(2)}) copy-start(s32[1,256]{1,0:T(1,128)} %parent_map.1) | copy-start | bytes 3076
  0.6 2.0 %copy-start.4 = (s32[1,256]{1,0:T(1,128)S(1)}, s32[1,256]{1,0:T(1,128)}, u32[]{:S(2)}) copy-start(s32[1,256]{1,0:T(1,128)} %leaf_map.1) | copy-start | bytes 3076
  0.7 2.0 %copy-start.3 = (bf16[1,64,256]{2,1,0:T(8,128)(2,1)S(1)}, bf16[1,64,256]{2,1,0:T(8,128)(2,1)}, u32[]{:S(2)}) copy-start(bf16[1,64,256]{2,1,0:T(8,128)(2,1)} %own_two.1) | copy-start | bytes 98308
  0.7 2.0 %copy-start.2 = (bf16[1,64,256]{2,1,0:T(8,128)(2,1)S(1)}, bf16[1,64,256]{2,1,0:T(8,128)(2,1)}, u32[]{:S(2)}) copy-start(bf16[1,64,256]{2,1,0:T(8,128)(2,1)} %own_one.1) | copy-start | bytes 98308
  0.7 2.0 %copy-start.1 = (bf16[1,4096,256]{2,1,0:T(8,128)(2,1)S(1)}, bf16[1,4096,256]{2,1,0:T(8,128)(2,1)}, u32[]{:S(2)}) copy-start(bf16[1,4096,256]{2,1,0:T(8,128)(2,1)} %omega.1) | copy-start | bytes 6291460
  0.7 2.3 %copy-start = (bf16[1,256,4096]{2,1,0:T(8,128)(2,1)S(1)}, bf16[1,256,4096]{2,1,0:T(8,128)(2,1)}, u32[]{:S(2)}) copy-start(bf16[1,256,4096]{2,1,0:T(8,128)(2,1)} %fronts.1) | copy-start | bytes 6291460

commit v7 on v6

--- a/solution.py
+++ b/solution.py
@@ -6,6 +6,7 @@
 from jax.sharding import Mesh, PartitionSpec as P
 
 DIGIT = 32
+LANES = 128
 CODE_ROWS = 16
 LIMIT = 32 * 2**20
 
@@ -34,7 +35,7 @@
     digits = jnp.where(line < 2, leaf, parent)
     digits = jnp.where(line % 2 == 0, digits >> 5, digits & (DIGIT - 1))
     code[...] = (digits.astype(jnp.float32) + blank[...]).astype(jnp.bfloat16)
-    lower[...] = picks((core, 1 - core), leaf)
+    lower[...] = picks((core,), leaf)
 
 
 def product_kernel(fronts, omega, own_one, own_two, code, out, rest, two):
@@ -62,14 +63,21 @@
     n_row = rows // block
     core, row, here = lax.axis_index("core"), lax.axis_index("row"), lax.axis_index("y")
     other = both.at[1 - core]
-    codes = mine[rows + block :, :], other[rows + block :, :]
-    (leaf, parent), (other_leaf, other_parent) = decode(codes[0]), decode(codes[1])
-    other_lower = picks((core, 1 - core), other_leaf)
-    table = jnp.concatenate(codes, axis=1)
+    leaf, parent = decode(mine[rows + block :, :])
+    other_leaf, other_parent = decode(other[rows + block :, :])
+    other_lower = picks((core,), other_leaf)
+    pages = [jnp.broadcast_to(half[:, k : k + LANES], (8, LANES)) for half in (parent, other_parent) for k in range(0, rows, LANES)]
     targets = []
-    for index, pick in ((leaf, lower[...]), (other_leaf, other_lower)):
-        _, target = decode(jnp.dot(table, pick, preferred_element_type=jnp.float32))
-        targets.append(jnp.where(index >= 0, target, -1))
+    for index in (leaf, other_leaf):
+        found = []
+        for k in range(0, rows, LANES):
+            at = jnp.broadcast_to(jnp.bitwise_xor(index[:, k : k + LANES], core * rows), (8, LANES))
+            value = jnp.full((8, LANES), -1, jnp.int32)
+            for page, entries in enumerate(pages):
+                entry = jnp.take_along_axis(entries, at & (LANES - 1), axis=1, mode="promise_in_bounds")
+                value = jnp.where(at >> 7 == page, entry, value)
+            found.append(value[:1])
+        targets.append(jnp.concatenate(found, axis=1))
     own = []
     for index in (parent, other_parent):
         turned = pltpu.roll(jnp.broadcast_to(index, (8, rows)), lax.rem(n_row - row, n_row) * block, 1)
@@ -77,7 +85,7 @@
     own = jnp.concatenate(own, axis=1)
     line = lax.broadcasted_iota(jnp.int32, (rows, 2 * block), 0)
     partial = jnp.concatenate([mine[:rows, :], rest[...], other[:rows, :]], axis=0)
-    pick = jnp.concatenate([lower[:rows], lower[:rows], other_lower[:rows]], axis=1)
+    pick = jnp.concatenate([lower[...], lower[...], other_lower], axis=1)
     level_one = jnp.dot(pick, partial, preferred_element_type=jnp.float32).astype(jnp.bfloat16)
     for x in range(n_row):
         out[2 * x + here, block:, :] = level_one[x * block : (x + 1) * block]
@@ -129,7 +137,7 @@
         cost_estimate=pl.CostEstimate(flops=8 * 10**9, bytes_accessed=2**24, transcendentals=0),
         name="first",
     )()
-    pick = pltpu.VMEM((2 * rows, rows), jnp.bfloat16)
+    pick = pltpu.VMEM((rows, rows), jnp.bfloat16)
     code, lower = pl.pallas_call(
         index_kernel,
         out_shape=(pltpu.VMEM((CODE_ROWS, rows), jnp.bfloat16), pick),

time: 25.5 us -> 25.5 us (level)
  no operation moved by 1% of the time
where the time goes in v7:
time: 25.5 us; the launch traced here: 25.3 us
  blocking collectives  20.3 us (80%)
  between operations  2.64 us (10%)
  Pallas kernels  2.02 us (8%)
  local copies, waits for them, and re-layouts  0.29 us (1%)
    all_to_all x1, blocking collectives, body(): pieces = lax.all_to_all(pieces, ('row', 'y'), 0, 0)  11.8 us
    all_gather x1, blocking collectives, body(): both = lax.all_gather(message, 'core')  8.56 us
    pallas_call x1, Pallas kernels, body(): pl.pallas_call(product_kernel, out_shape=(pltpu.VMEM((rows + block + CODE...  0.71 us
    pallas_call x1, Pallas kernels, body(): pl.pallas_call(sum_kernel, out_shape=(shape, shape), in_specs=[vmem, vmem...  0.7 us
    pallas_call x1, Pallas kernels, body(): pl.pallas_call(place_kernel, out_shape=pltpu.VMEM((2 * n_row, 2 * block,...  0.57 us

profile of v7, /device:TPU:1, one launch (start us, length us, event | category | flops | bytes accessed | tf_op | source)
XLA Modules:
  0.0 25.3 jit_solution(16889266703339229570)
XLA Ops:
  0.6 0.0 copy-start.5
  0.6 0.0 copy-start.4
  0.7 0.0 copy-start.3
  0.7 0.0 copy-start.2
  0.7 0.0 copy-start.1
  0.7 0.0 copy-start
  2.6 0.0 copy-done.5
  2.6 0.0 copy-done.4
  2.7 0.0 copy-done.3
  2.7 0.0 copy-done.2
  2.7 0.0 copy-done.1
  2.7 0.3 %copy-done = bf16[1,256,4096]{2,1,0:T(8,128)(2,1)S(1)} copy-done((bf16[1,256,4096]{2,1,0:T(8,128)(2,1)S(1)}, bf16[1,256,4096]{2,1,0:T(8,128)(2,1)}, u32[]{:S(2)}) %copy-start) | copy-done | bytes 2097176
  3.0 0.7 %product.1 = (bf16[336,256]{1,0:T(8,128)(2,1)S(1)}, bf16[256,256]{1,0:T(8,128)(2,1)S(1)}, bf16[64,256]{1,0:T(8,128)(2,1)S(1)}) custom-call(bf16[1,256,4096]{2,1,0:T(8,128)(2,1)S(1)} %copy-done, bf16[1,4096,256]{2,1,0:T(8,128)(2,1)S(1)} %copy-done.1, bf16[1,64,256]{2,1,0:T(8,128)(2,1)S(1)} %copy-done.2, bf16[1,64,256]{2,1,0:T(8,128)(2,1)S(1)} %copy-done.3, ...), custom_call_target="tpu_custom_call" | custom-call | tf_op jit(solution)/shard_map/product/pallas_call | solution.py:149
  3.7 8.6 %all-gather = bf16[672,256]{1,0:T(8,128)(2,1)S(1)} all-gather(bf16[336,256]{1,0:T(8,128)(2,1)S(1)} %get-tuple-element.8.mine.message), channel_id=2, replica_groups=mesh['group'=32,'y'=2,'core'=2,'row'=4] {'core'}, dimensions={0}, use_global_device_ids=true | all-gather | bytes 516096 | tf_op jit(solution)/shard_map/all_gather | solution.py:161
  12.2 0.6 %place.1 = bf16[8,128,256]{2,1,0:T(8,128)(2,1)S(1)} custom-call(bf16[336,256]{1,0:T(8,128)(2,1)S(1)} %get-tuple-element.8.mine.message, bf16[256,256]{1,0:T(8,128)(2,1)S(1)} %get-tuple-element.9.rest, bf16[2,336,256]{2,1,0:T(8,128)(2,1)S(1)} %bitcast.1, bf16[256,256]{1,0:T(8,128)(2,1)S(1)} %get-tuple-element.10.lower), custom_call_target="tpu_custom_call" | custom-call | tf_op jit(solution)/shard_map/place/pallas_call | solution.py:162
  12.8 11.8 %all_to_all.5.pieces = bf16[8,128,256]{2,1,0:T(8,128)(2,1)S(1)} all-to-all(bf16[8,128,256]{2,1,0:T(8,128)(2,1)S(1)} %place.1), channel_id=1, replica_groups=mesh['group'=32,'y'=2,'core'=2,'row'=4] {'row','y'}, dimensions={0} | all-to-all | bytes 1048576 | tf_op jit(solution)/shard_map/all_to_all | solution.py:170
  24.6 0.7 %total.1 = (bf16[1,64,256]{2,1,0:T(8,128)(2,1)}, bf16[1,64,256]{2,1,0:T(8,128)(2,1)}) custom-call(bf16[8,128,256]{2,1,0:T(8,128)(2,1)S(1)} %all_to_all.5.pieces, bf16[336,256]{1,0:T(8,128)(2,1)S(1)} %get-tuple-element.8.mine.message, bf16[64,256]{1,0:T(8,128)(2,1)S(1)} %get-tuple-element.11.own_two), custom_call_target="tpu_custom_call" | custom-call | tf_op jit(solution)/shard_map/total/pallas_call | solution.py:172
  (2 shorter events, 0.0 us)
Async XLA Ops:
  0.6 2.0 %copy-start.5 = (s32[1,256]{1,0:T(1,128)S(1)}, s32[1,256]{1,0:T(1,128)}, u32[]{:S(2)}) copy-start(s32[1,256]{1,0:T(1,128)} %parent_map.1) | copy-start | bytes 3076
  0.6 2.0 %copy-start.4 = (s32[1,256]{1,0:T(1,128)S(1)}, s32[1,256]{1,0:T(1,128)}, u32[]{:S(2)}) copy-start(s32[1,256]{1,0:T(1,128)} %leaf_map.1) | copy-start | bytes 3076
  0.7 2.0 %copy-start.3 = (bf16[1,64,256]{2,1,0:T(8,128)(2,1)S(1)}, bf16[1,64,256]{2,1,0:T(8,128)(2,1)}, u32[]{:S(2)}) copy-start(bf16[1,64,256]{2,1,0:T(8,128)(2,1)} %own_two.1) | copy-start | bytes 98308
  0.7 2.0 %copy-start.2 = (bf16[1,64,256]{2,1,0:T(8,128)(2,1)S(1)}, bf16[1,64,256]{2,1,0:T(8,128)(2,1)}, u32[]{:S(2)}) copy-start(bf16[1,64,256]{2,1,0:T(8,128)(2,1)} %own_one.1) | copy-start | bytes 98308
  0.7 2.0 %copy-start.1 = (bf16[1,4096,256]{2,1,0:T(8,128)(2,1)S(1)}, bf16[1,4096,256]{2,1,0:T(8,128)(2,1)}, u32[]{:S(2)}) copy-start(bf16[1,4096,256]{2,1,0:T(8,128)(2,1)} %omega.1) | copy-start | bytes 6291460
  0.7 2.3 %copy-start = (bf16[1,256,4096]{2,1,0:T(8,128)(2,1)S(1)}, bf16[1,256,4096]{2,1,0:T(8,128)(2,1)}, u32[]{:S(2)}) copy-start(bf16[1,256,4096]{2,1,0:T(8,128)(2,1)} %fronts.1) | copy-start | bytes 6291460

commit v8 on v7

--- a/solution.py
+++ b/solution.py
@@ -7,6 +7,7 @@
 
 DIGIT = 32
 LANES = 128
+TIER = 64
 CODE_ROWS = 16
 LIMIT = 32 * 2**20
 
@@ -38,16 +39,28 @@
     lower[...] = picks((core,), leaf)
 
 
-def product_kernel(fronts, omega, own_one, own_two, code, out, rest, two):
+def product_kernel(fronts, omega, own_one, own_two, code, leaf_size, out, rest, two):
     rows = fronts.shape[1]
     mine = own_one.shape[1]
     out[rows : rows + mine, :] = own_one[0]
     out[rows + mine :, :] = code[...]
     two[...] = own_two[0]
-    partial = jnp.dot(fronts[0], omega[0], preferred_element_type=jnp.float32)
-    high = partial.astype(jnp.bfloat16)
-    out[:rows, :] = high
-    rest[...] = (partial - high.astype(jnp.float32)).astype(jnp.bfloat16)
+
+    def multiply(live):
+        partial = jnp.dot(fronts[0, :live, :], omega[0], preferred_element_type=jnp.float32)
+        high = partial.astype(jnp.bfloat16)
+        out[:live, :] = high
+        rest[:live, :] = (partial - high.astype(jnp.float32)).astype(jnp.bfloat16)
+        if live < rows:
+            dead = jnp.zeros((rows - live, out.shape[1]), jnp.bfloat16)
+            out[live:rows, :] = dead
+            rest[live:, :] = dead
+
+    size = leaf_size[0]
+    for live in range(2 * TIER, rows + 1, TIER):
+        above = live - TIER if live > 2 * TIER else -1
+        wanted = size <= live if live < rows else size > above
+        pl.when(jnp.logical_and(size > above, wanted))(lambda live=live: multiply(live))
 
 
 def decode(code):
@@ -153,11 +166,11 @@
             pltpu.VMEM((rows, cols), jnp.bfloat16),
             pltpu.VMEM((block, cols), jnp.bfloat16),
         ),
-        in_specs=[vmem] * 5,
+        in_specs=[vmem] * 5 + [smem],
         out_specs=(vmem,) * 3,
         compiler_params=params,
         name="product",
-    )(fronts, omega, own_one, own_two, near(code))
+    )(fronts, omega, own_one, own_two, near(code), leaf_sizes)
     both = lax.all_gather(message, "core")
     pieces = pl.pallas_call(
         place_kernel,

time: 25.5 us -> 25.4 us (level)
  no operation moved by 1% of the time
where the time goes in v8:
time: 25.4 us; the launch traced here: 25.3 us
  blocking collectives  20.3 us (80%)
  between operations  2.64 us (10%)
  Pallas kernels  2.02 us (8%)
  local copies, waits for them, and re-layouts  0.29 us (1%)
    all_to_all x1, blocking collectives, body(): pieces = lax.all_to_all(pieces, ('row', 'y'), 0, 0)  11.8 us
    all_gather x1, blocking collectives, body(): both = lax.all_gather(message, 'core')  8.56 us
    pallas_call x1, Pallas kernels, body(): pl.pallas_call(product_kernel, out_shape=(pltpu.VMEM((rows + block + CODE...  0.71 us
    pallas_call x1, Pallas kernels, body(): pl.pallas_call(sum_kernel, out_shape=(shape, shape), in_specs=[vmem, vmem...  0.7 us
    pallas_call x1, Pallas kernels, body(): pl.pallas_call(place_kernel, out_shape=pltpu.VMEM((2 * n_row, 2 * block,...  0.57 us

profile of v8, /device:TPU:1, one launch (start us, length us, event | category | flops | bytes accessed | tf_op | source)
XLA Modules:
  0.0 25.3 jit_solution(8791889388849331321)
XLA Ops:
  0.6 0.0 copy-start.5
  0.6 0.0 copy-start.4
  0.7 0.0 copy-start.3
  0.7 0.0 copy-start.2
  0.7 0.0 copy-start.1
  0.7 0.0 copy-start
  2.6 0.0 copy-done.5
  2.6 0.0 copy-done.4
  2.7 0.0 copy-done.3
  2.7 0.0 copy-done.2
  2.7 0.0 copy-done.1
  2.7 0.3 %copy-done = bf16[1,256,4096]{2,1,0:T(8,128)(2,1)S(1)} copy-done((bf16[1,256,4096]{2,1,0:T(8,128)(2,1)S(1)}, bf16[1,256,4096]{2,1,0:T(8,128)(2,1)}, u32[]{:S(2)}) %copy-start) | copy-done | bytes 2097176
  3.0 0.7 %product.1 = (bf16[336,256]{1,0:T(8,128)(2,1)S(1)}, bf16[256,256]{1,0:T(8,128)(2,1)S(1)}, bf16[64,256]{1,0:T(8,128)(2,1)S(1)}) custom-call(bf16[1,256,4096]{2,1,0:T(8,128)(2,1)S(1)} %copy-done, bf16[1,4096,256]{2,1,0:T(8,128)(2,1)S(1)} %copy-done.1, bf16[1,64,256]{2,1,0:T(8,128)(2,1)S(1)} %copy-done.2, bf16[1,64,256]{2,1,0:T(8,128)(2,1)S(1)} %copy-done.3, ...), custom_call_target="tpu_custom_call" | custom-call | tf_op jit(solution)/shard_map/product/pallas_call | solution.py:162
  3.7 8.6 %all-gather = bf16[672,256]{1,0:T(8,128)(2,1)S(1)} all-gather(bf16[336,256]{1,0:T(8,128)(2,1)S(1)} %get-tuple-element.8.mine.message), channel_id=2, replica_groups=mesh['group'=32,'y'=2,'core'=2,'row'=4] {'core'}, dimensions={0}, use_global_device_ids=true | all-gather | bytes 516096 | tf_op jit(solution)/shard_map/all_gather | solution.py:174
  12.2 0.6 %place.1 = bf16[8,128,256]{2,1,0:T(8,128)(2,1)S(1)} custom-call(bf16[336,256]{1,0:T(8,128)(2,1)S(1)} %get-tuple-element.8.mine.message, bf16[256,256]{1,0:T(8,128)(2,1)S(1)} %get-tuple-element.9.rest, bf16[2,336,256]{2,1,0:T(8,128)(2,1)S(1)} %bitcast.1, bf16[256,256]{1,0:T(8,128)(2,1)S(1)} %get-tuple-element.10.lower), custom_call_target="tpu_custom_call" | custom-call | tf_op jit(solution)/shard_map/place/pallas_call | solution.py:175
  12.8 11.8 %all_to_all.5.pieces = bf16[8,128,256]{2,1,0:T(8,128)(2,1)S(1)} all-to-all(bf16[8,128,256]{2,1,0:T(8,128)(2,1)S(1)} %place.1), channel_id=1, replica_groups=mesh['group'=32,'y'=2,'core'=2,'row'=4] {'row','y'}, dimensions={0} | all-to-all | bytes 1048576 | tf_op jit(solution)/shard_map/all_to_all | solution.py:183
  24.6 0.7 %total.1 = (bf16[1,64,256]{2,1,0:T(8,128)(2,1)}, bf16[1,64,256]{2,1,0:T(8,128)(2,1)}) custom-call(bf16[8,128,256]{2,1,0:T(8,128)(2,1)S(1)} %all_to_all.5.pieces, bf16[336,256]{1,0:T(8,128)(2,1)S(1)} %get-tuple-element.8.mine.message, bf16[64,256]{1,0:T(8,128)(2,1)S(1)} %get-tuple-element.11.own_two), custom_call_target="tpu_custom_call" | custom-call | tf_op jit(solution)/shard_map/total/pallas_call | solution.py:185
  (2 shorter events, 0.0 us)
Async XLA Ops:
  0.6 2.0 %copy-start.5 = (s32[1,256]{1,0:T(1,128)S(1)}, s32[1,256]{1,0:T(1,128)}, u32[]{:S(2)}) copy-start(s32[1,256]{1,0:T(1,128)} %parent_map.1) | copy-start | bytes 3076
  0.6 2.0 %copy-start.4 = (s32[1,256]{1,0:T(1,128)S(1)}, s32[1,256]{1,0:T(1,128)}, u32[]{:S(2)}) copy-start(s32[1,256]{1,0:T(1,128)} %leaf_map.1) | copy-start | bytes 3076
  0.7 2.0 %copy-start.3 = (bf16[1,64,256]{2,1,0:T(8,128)(2,1)S(1)}, bf16[1,64,256]{2,1,0:T(8,128)(2,1)}, u32[]{:S(2)}) copy-start(bf16[1,64,256]{2,1,0:T(8,128)(2,1)} %own_two.1) | copy-start | bytes 98308
  0.7 2.0 %copy-start.2 = (bf16[1,64,256]{2,1,0:T(8,128)(2,1)S(1)}, bf16[1,64,256]{2,1,0:T(8,128)(2,1)}, u32[]{:S(2)}) copy-start(bf16[1,64,256]{2,1,0:T(8,128)(2,1)} %own_one.1) | copy-start | bytes 98308
  0.7 2.0 %copy-start.1 = (bf16[1,4096,256]{2,1,0:T(8,128)(2,1)S(1)}, bf16[1,4096,256]{2,1,0:T(8,128)(2,1)}, u32[]{:S(2)}) copy-start(bf16[1,4096,256]{2,1,0:T(8,128)(2,1)} %omega.1) | copy-start | bytes 6291460
  0.7 2.3 %copy-start = (bf16[1,256,4096]{2,1,0:T(8,128)(2,1)S(1)}, bf16[1,256,4096]{2,1,0:T(8,128)(2,1)}, u32[]{:S(2)}) copy-start(bf16[1,256,4096]{2,1,0:T(8,128)(2,1)} %fronts.1) | copy-start | bytes 6291460

commit v9 on v8

--- a/solution.py
+++ b/solution.py
@@ -103,7 +103,7 @@
     for x in range(n_row):
         out[2 * x + here, block:, :] = level_one[x * block : (x + 1) * block]
     partial = jnp.concatenate([partial, mine[rows : rows + block, :], other[rows : rows + block, :]], axis=0)
-    for k, y in enumerate((here, 1 - here)):
+    for k, y in enumerate((1 - here, here)):
         quarter = core + 2 * y
         picked = picks((quarter,), targets[0])
         pick = [picked, picked, picks((quarter,), targets[1]), (line + quarter * rows == own).astype(jnp.bfloat16)]
@@ -111,7 +111,7 @@
         high = placed.astype(jnp.bfloat16)
         for x in range(n_row):
             out[2 * x + y, :block, :] = high[x * block : (x + 1) * block]
-        if k == 1:
+        if k == 0:
             low = (placed - high.astype(jnp.float32)).astype(jnp.bfloat16)
             for x in range(n_row):
                 out[2 * x + y, block:, :] = low[x * block : (x + 1) * block]

time: 25.4 us -> 25.2 us (level)
  Pallas kernels: 2.02 us -> 1.76 us
    pallas_call x1, Pallas kernels: 0.71 us -> 0.46 us  [body(): pl.pallas_call(product_kernel, out_shape=(pltpu.VMEM((rows + block + CODE...]
where the time goes in v9:
time: 25.2 us; the launch traced here: 25 us
  blocking collectives  20.3 us (81%)
  between operations  2.64 us (10%)
  Pallas kernels  1.76 us (7%)
  local copies, waits for them, and re-layouts  0.29 us (1%)
    all_to_all x1, blocking collectives, body(): pieces = lax.all_to_all(pieces, ('row', 'y'), 0, 0)  11.8 us
    all_gather x1, blocking collectives, body(): both = lax.all_gather(message, 'core')  8.57 us
    pallas_call x1, Pallas kernels, body(): pl.pallas_call(sum_kernel, out_shape=(shape, shape), in_specs=[vmem, vmem...  0.7 us
    pallas_call x1, Pallas kernels, body(): pl.pallas_call(place_kernel, out_shape=pltpu.VMEM((2 * n_row, 2 * block,...  0.56 us

profile of v9, /device:TPU:1, one launch (start us, length us, event | category | flops | bytes accessed | tf_op | source)
XLA Modules:
  0.0 25.0 jit_solution(7664149225601241076)
XLA Ops:
  0.6 0.0 copy-start.5
  0.6 0.0 copy-start.4
  0.7 0.0 copy-start.3
  0.7 0.0 copy-start.2
  0.7 0.0 copy-start.1
  0.7 0.0 copy-start
  2.6 0.0 copy-done.5
  2.6 0.0 copy-done.4
  2.7 0.0 copy-done.3
  2.7 0.0 copy-done.2
  2.7 0.0 copy-done.1
  2.7 0.3 %copy-done = bf16[1,256,4096]{2,1,0:T(8,128)(2,1)S(1)} copy-done((bf16[1,256,4096]{2,1,0:T(8,128)(2,1)S(1)}, bf16[1,256,4096]{2,1,0:T(8,128)(2,1)}, u32[]{:S(2)}) %copy-start) | copy-done | bytes 2097176
  3.0 0.5 %product.1 = (bf16[336,256]{1,0:T(8,128)(2,1)S(1)}, bf16[256,256]{1,0:T(8,128)(2,1)S(1)}, bf16[64,256]{1,0:T(8,128)(2,1)S(1)}) custom-call(bf16[1,256,4096]{2,1,0:T(8,128)(2,1)S(1)} %copy-done, bf16[1,4096,256]{2,1,0:T(8,128)(2,1)S(1)} %copy-done.1, bf16[1,64,256]{2,1,0:T(8,128)(2,1)S(1)} %copy-done.2, bf16[1,64,256]{2,1,0:T(8,128)(2,1)S(1)} %copy-done.3, ...), custom_call_target="tpu_custom_call" | custom-call | tf_op jit(solution)/shard_map/product/pallas_call | solution.py:162
  3.4 8.6 %all-gather = bf16[672,256]{1,0:T(8,128)(2,1)S(1)} all-gather(bf16[336,256]{1,0:T(8,128)(2,1)S(1)} %get-tuple-element.8.mine.message), channel_id=2, replica_groups=mesh['group'=32,'y'=2,'core'=2,'row'=4] {'core'}, dimensions={0}, use_global_device_ids=true | all-gather | bytes 516096 | tf_op jit(solution)/shard_map/all_gather | solution.py:174
  12.0 0.6 %place.1 = bf16[8,128,256]{2,1,0:T(8,128)(2,1)S(1)} custom-call(bf16[336,256]{1,0:T(8,128)(2,1)S(1)} %get-tuple-element.8.mine.message, bf16[256,256]{1,0:T(8,128)(2,1)S(1)} %get-tuple-element.9.rest, bf16[2,336,256]{2,1,0:T(8,128)(2,1)S(1)} %bitcast.1, bf16[256,256]{1,0:T(8,128)(2,1)S(1)} %get-tuple-element.10.lower), custom_call_target="tpu_custom_call" | custom-call | tf_op jit(solution)/shard_map/place/pallas_call | solution.py:175
  12.6 11.8 %all_to_all.5.pieces = bf16[8,128,256]{2,1,0:T(8,128)(2,1)S(1)} all-to-all(bf16[8,128,256]{2,1,0:T(8,128)(2,1)S(1)} %place.1), channel_id=1, replica_groups=mesh['group'=32,'y'=2,'core'=2,'row'=4] {'row','y'}, dimensions={0} | all-to-all | bytes 1048576 | tf_op jit(solution)/shard_map/all_to_all | solution.py:183
  24.3 0.7 %total.1 = (bf16[1,64,256]{2,1,0:T(8,128)(2,1)}, bf16[1,64,256]{2,1,0:T(8,128)(2,1)}) custom-call(bf16[8,128,256]{2,1,0:T(8,128)(2,1)S(1)} %all_to_all.5.pieces, bf16[336,256]{1,0:T(8,128)(2,1)S(1)} %get-tuple-element.8.mine.message, bf16[64,256]{1,0:T(8,128)(2,1)S(1)} %get-tuple-element.11.own_two), custom_call_target="tpu_custom_call" | custom-call | tf_op jit(solution)/shard_map/total/pallas_call | solution.py:185
  (2 shorter events, 0.0 us)
Async XLA Ops:
  0.6 2.0 %copy-start.5 = (s32[1,256]{1,0:T(1,128)S(1)}, s32[1,256]{1,0:T(1,128)}, u32[]{:S(2)}) copy-start(s32[1,256]{1,0:T(1,128)} %parent_map.1) | copy-start | bytes 3076
  0.6 2.0 %copy-start.4 = (s32[1,256]{1,0:T(1,128)S(1)}, s32[1,256]{1,0:T(1,128)}, u32[]{:S(2)}) copy-start(s32[1,256]{1,0:T(1,128)} %leaf_map.1) | copy-start | bytes 3076
  0.7 2.0 %copy-start.3 = (bf16[1,64,256]{2,1,0:T(8,128)(2,1)S(1)}, bf16[1,64,256]{2,1,0:T(8,128)(2,1)}, u32[]{:S(2)}) copy-start(bf16[1,64,256]{2,1,0:T(8,128)(2,1)} %own_two.1) | copy-start | bytes 98308
  0.7 2.0 %copy-start.2 = (bf16[1,64,256]{2,1,0:T(8,128)(2,1)S(1)}, bf16[1,64,256]{2,1,0:T(8,128)(2,1)}, u32[]{:S(2)}) copy-start(bf16[1,64,256]{2,1,0:T(8,128)(2,1)} %own_one.1) | copy-start | bytes 98308
  0.7 2.0 %copy-start.1 = (bf16[1,4096,256]{2,1,0:T(8,128)(2,1)S(1)}, bf16[1,4096,256]{2,1,0:T(8,128)(2,1)}, u32[]{:S(2)}) copy-start(bf16[1,4096,256]{2,1,0:T(8,128)(2,1)} %omega.1) | copy-start | bytes 6291460
  0.7 2.3 %copy-start = (bf16[1,256,4096]{2,1,0:T(8,128)(2,1)S(1)}, bf16[1,256,4096]{2,1,0:T(8,128)(2,1)}, u32[]{:S(2)}) copy-start(bf16[1,256,4096]{2,1,0:T(8,128)(2,1)} %fronts.1) | copy-start | bytes 6291460

commit v10 on v7

--- a/solution.py
+++ b/solution.py
@@ -90,7 +90,7 @@
     for x in range(n_row):
         out[2 * x + here, block:, :] = level_one[x * block : (x + 1) * block]
     partial = jnp.concatenate([partial, mine[rows : rows + block, :], other[rows : rows + block, :]], axis=0)
-    for k, y in enumerate((here, 1 - here)):
+    for k, y in enumerate((1 - here, here)):
         quarter = core + 2 * y
         picked = picks((quarter,), targets[0])
         pick = [picked, picked, picks((quarter,), targets[1]), (line + quarter * rows == own).astype(jnp.bfloat16)]
@@ -98,7 +98,7 @@
         high = placed.astype(jnp.bfloat16)
         for x in range(n_row):
             out[2 * x + y, :block, :] = high[x * block : (x + 1) * block]
-        if k == 1:
+        if k == 0:
             low = (placed - high.astype(jnp.float32)).astype(jnp.bfloat16)
             for x in range(n_row):
                 out[2 * x + y, block:, :] = low[x * block : (x + 1) * block]

time: 25.5 us -> 25.4 us (level)
  no operation moved by 1% of the time
where the time goes in v10:
time: 25.4 us; the launch traced here: 25.3 us
  blocking collectives  20.3 us (80%)
  between operations  2.64 us (10%)
  Pallas kernels  2.01 us (8%)
  local copies, waits for them, and re-layouts  0.29 us (1%)
    all_to_all x1, blocking collectives, body(): pieces = lax.all_to_all(pieces, ('row', 'y'), 0, 0)  11.8 us
    all_gather x1, blocking collectives, body(): both = lax.all_gather(message, 'core')  8.56 us
    pallas_call x1, Pallas kernels, body(): pl.pallas_call(product_kernel, out_shape=(pltpu.VMEM((rows + block + CODE...  0.71 us
    pallas_call x1, Pallas kernels, body(): pl.pallas_call(sum_kernel, out_shape=(shape, shape), in_specs=[vmem, vmem...  0.7 us
    pallas_call x1, Pallas kernels, body(): pl.pallas_call(place_kernel, out_shape=pltpu.VMEM((2 * n_row, 2 * block,...  0.56 us

profile of v10, /device:TPU:1, one launch (start us, length us, event | category | flops | bytes accessed | tf_op | source)
XLA Modules:
  0.0 25.3 jit_solution(6228277121863679327)
XLA Ops:
  0.6 0.0 copy-start.5
  0.6 0.0 copy-start.4
  0.7 0.0 copy-start.3
  0.7 0.0 copy-start.2
  0.7 0.0 copy-start.1
  0.7 0.0 copy-start
  2.6 0.0 copy-done.5
  2.6 0.0 copy-done.4
  2.7 0.0 copy-done.3
  2.7 0.0 copy-done.2
  2.7 0.0 copy-done.1
  2.7 0.3 %copy-done = bf16[1,256,4096]{2,1,0:T(8,128)(2,1)S(1)} copy-done((bf16[1,256,4096]{2,1,0:T(8,128)(2,1)S(1)}, bf16[1,256,4096]{2,1,0:T(8,128)(2,1)}, u32[]{:S(2)}) %copy-start) | copy-done | bytes 2097176
  3.0 0.7 %product.1 = (bf16[336,256]{1,0:T(8,128)(2,1)S(1)}, bf16[256,256]{1,0:T(8,128)(2,1)S(1)}, bf16[64,256]{1,0:T(8,128)(2,1)S(1)}) custom-call(bf16[1,256,4096]{2,1,0:T(8,128)(2,1)S(1)} %copy-done, bf16[1,4096,256]{2,1,0:T(8,128)(2,1)S(1)} %copy-done.1, bf16[1,64,256]{2,1,0:T(8,128)(2,1)S(1)} %copy-done.2, bf16[1,64,256]{2,1,0:T(8,128)(2,1)S(1)} %copy-done.3, ...), custom_call_target="tpu_custom_call" | custom-call | tf_op jit(solution)/shard_map/product/pallas_call | solution.py:149
  3.7 8.6 %all-gather = bf16[672,256]{1,0:T(8,128)(2,1)S(1)} all-gather(bf16[336,256]{1,0:T(8,128)(2,1)S(1)} %get-tuple-element.8.mine.message), channel_id=2, replica_groups=mesh['group'=32,'y'=2,'core'=2,'row'=4] {'core'}, dimensions={0}, use_global_device_ids=true | all-gather | bytes 516096 | tf_op jit(solution)/shard_map/all_gather | solution.py:161
  12.2 0.6 %place.1 = bf16[8,128,256]{2,1,0:T(8,128)(2,1)S(1)} custom-call(bf16[336,256]{1,0:T(8,128)(2,1)S(1)} %get-tuple-element.8.mine.message, bf16[256,256]{1,0:T(8,128)(2,1)S(1)} %get-tuple-element.9.rest, bf16[2,336,256]{2,1,0:T(8,128)(2,1)S(1)} %bitcast.1, bf16[256,256]{1,0:T(8,128)(2,1)S(1)} %get-tuple-element.10.lower), custom_call_target="tpu_custom_call" | custom-call | tf_op jit(solution)/shard_map/place/pallas_call | solution.py:162
  12.8 11.8 %all_to_all.5.pieces = bf16[8,128,256]{2,1,0:T(8,128)(2,1)S(1)} all-to-all(bf16[8,128,256]{2,1,0:T(8,128)(2,1)S(1)} %place.1), channel_id=1, replica_groups=mesh['group'=32,'y'=2,'core'=2,'row'=4] {'row','y'}, dimensions={0} | all-to-all | bytes 1048576 | tf_op jit(solution)/shard_map/all_to_all | solution.py:170
  24.6 0.7 %total.1 = (bf16[1,64,256]{2,1,0:T(8,128)(2,1)}, bf16[1,64,256]{2,1,0:T(8,128)(2,1)}) custom-call(bf16[8,128,256]{2,1,0:T(8,128)(2,1)S(1)} %all_to_all.5.pieces, bf16[336,256]{1,0:T(8,128)(2,1)S(1)} %get-tuple-element.8.mine.message, bf16[64,256]{1,0:T(8,128)(2,1)S(1)} %get-tuple-element.11.own_two), custom_call_target="tpu_custom_call" | custom-call | tf_op jit(solution)/shard_map/total/pallas_call | solution.py:172
  (2 shorter events, 0.0 us)
Async XLA Ops:
  0.6 2.0 %copy-start.5 = (s32[1,256]{1,0:T(1,128)S(1)}, s32[1,256]{1,0:T(1,128)}, u32[]{:S(2)}) copy-start(s32[1,256]{1,0:T(1,128)} %parent_map.1) | copy-start | bytes 3076
  0.6 2.0 %copy-start.4 = (s32[1,256]{1,0:T(1,128)S(1)}, s32[1,256]{1,0:T(1,128)}, u32[]{:S(2)}) copy-start(s32[1,256]{1,0:T(1,128)} %leaf_map.1) | copy-start | bytes 3076
  0.7 2.0 %copy-start.3 = (bf16[1,64,256]{2,1,0:T(8,128)(2,1)S(1)}, bf16[1,64,256]{2,1,0:T(8,128)(2,1)}, u32[]{:S(2)}) copy-start(bf16[1,64,256]{2,1,0:T(8,128)(2,1)} %own_two.1) | copy-start | bytes 98308
  0.7 2.0 %copy-start.2 = (bf16[1,64,256]{2,1,0:T(8,128)(2,1)S(1)}, bf16[1,64,256]{2,1,0:T(8,128)(2,1)}, u32[]{:S(2)}) copy-start(bf16[1,64,256]{2,1,0:T(8,128)(2,1)} %own_one.1) | copy-start | bytes 98308
  0.7 2.0 %copy-start.1 = (bf16[1,4096,256]{2,1,0:T(8,128)(2,1)S(1)}, bf16[1,4096,256]{2,1,0:T(8,128)(2,1)}, u32[]{:S(2)}) copy-start(bf16[1,4096,256]{2,1,0:T(8,128)(2,1)} %omega.1) | copy-start | bytes 6291460
  0.7 2.3 %copy-start = (bf16[1,256,4096]{2,1,0:T(8,128)(2,1)S(1)}, bf16[1,256,4096]{2,1,0:T(8,128)(2,1)}, u32[]{:S(2)}) copy-start(bf16[1,256,4096]{2,1,0:T(8,128)(2,1)} %fronts.1) | copy-start | bytes 6291460

commit v11 on v7

--- a/solution.py
+++ b/solution.py
@@ -38,12 +38,11 @@
     lower[...] = picks((core,), leaf)
 
 
-def product_kernel(fronts, omega, own_one, own_two, code, out, rest, two):
+def product_kernel(fronts, omega, own_one, code, out, rest):
     rows = fronts.shape[1]
     mine = own_one.shape[1]
     out[rows : rows + mine, :] = own_one[0]
     out[rows + mine :, :] = code[...]
-    two[...] = own_two[0]
     partial = jnp.dot(fronts[0], omega[0], preferred_element_type=jnp.float32)
     high = partial.astype(jnp.bfloat16)
     out[:rows, :] = high
@@ -106,13 +105,13 @@
 
 def sum_kernel(pieces, message, own_two, one, two):
     n_row, rows = pieces.shape[0] // 2, pieces.shape[2]
-    block = own_two.shape[0]
+    block = own_two.shape[1]
     y = lax.axis_index("y")
     total = message[rows : rows + block, :].astype(jnp.float32)
     for x in range(n_row):
         total += pieces[2 * x + y, block:, :].astype(jnp.float32)
     one[0] = total.astype(jnp.bfloat16)
-    total = own_two[...].astype(jnp.float32)
+    total = own_two[0].astype(jnp.float32)
     for k in range(2 * n_row):
         total += pieces[k, :block, :].astype(jnp.float32)
     for x in range(n_row):
@@ -146,18 +145,17 @@
         compiler_params=params,
         name="index",
     )(near(blank), leaf_map, parent_map, leaf_sizes, parent_count)
-    message, rest, late = pl.pallas_call(
+    message, rest = pl.pallas_call(
         product_kernel,
         out_shape=(
             pltpu.VMEM((rows + block + CODE_ROWS, cols), jnp.bfloat16),
             pltpu.VMEM((rows, cols), jnp.bfloat16),
-            pltpu.VMEM((block, cols), jnp.bfloat16),
         ),
-        in_specs=[vmem] * 5,
-        out_specs=(vmem,) * 3,
+        in_specs=[vmem] * 4,
+        out_specs=(vmem,) * 2,
         compiler_params=params,
         name="product",
-    )(fronts, omega, own_one, own_two, near(code))
+    )(fronts, omega, own_one, near(code))
     both = lax.all_gather(message, "core")
     pieces = pl.pallas_call(
         place_kernel,
@@ -176,7 +174,7 @@
         out_specs=(vmem, vmem),
         compiler_params=params,
         name="total",
-    )(near(pieces), near(message), near(late))
+    )(near(pieces), near(message), own_two)
 
 
 def solution(mesh):

time: 25.5 us -> 25.5 us (level)
  no operation moved by 1% of the time
where the time goes in v11:
time: 25.5 us; the launch traced here: 25.3 us
  blocking collectives  20.3 us (80%)
  between operations  2.62 us (10%)
  Pallas kernels  2.02 us (8%)
  local copies, waits for them, and re-layouts  0.3 us (1%)
    all_to_all x1, blocking collectives, body(): pieces = lax.all_to_all(pieces, ('row', 'y'), 0, 0)  11.8 us
    all_gather x1, blocking collectives, body(): both = lax.all_gather(message, 'core')  8.56 us
    pallas_call x1, Pallas kernels, body(): pl.pallas_call(product_kernel, out_shape=(pltpu.VMEM((rows + block + CODE...  0.71 us
    pallas_call x1, Pallas kernels, body(): pl.pallas_call(sum_kernel, out_shape=(shape, shape), in_specs=[vmem, vmem...  0.7 us
    pallas_call x1, Pallas kernels, body(): pl.pallas_call(place_kernel, out_shape=pltpu.VMEM((2 * n_row, 2 * block,...  0.57 us

profile of v11, /device:TPU:1, one launch (start us, length us, event | category | flops | bytes accessed | tf_op | source)
XLA Modules:
  0.0 25.3 jit_solution(6483009823921155708)
XLA Ops:
  0.6 0.0 copy-start.5
  0.6 0.0 copy-start.4
  0.7 0.0 copy-start.2
  0.7 0.0 copy-start.1
  0.7 0.0 copy-start
  2.6 0.0 copy-done.5
  2.6 0.0 copy-done.4
  2.6 0.0 copy-done.2
  2.7 0.0 copy-done.1
  2.7 0.3 %copy-done = bf16[1,256,4096]{2,1,0:T(8,128)(2,1)S(1)} copy-done((bf16[1,256,4096]{2,1,0:T(8,128)(2,1)S(1)}, bf16[1,256,4096]{2,1,0:T(8,128)(2,1)}, u32[]{:S(2)}) %copy-start) | copy-done | bytes 2097176
  2.9 0.7 %product.1 = (bf16[336,256]{1,0:T(8,128)(2,1)S(1)}, bf16[256,256]{1,0:T(8,128)(2,1)S(1)}) custom-call(bf16[1,256,4096]{2,1,0:T(8,128)(2,1)S(1)} %copy-done, bf16[1,4096,256]{2,1,0:T(8,128)(2,1)S(1)} %copy-done.1, bf16[1,64,256]{2,1,0:T(8,128)(2,1)S(1)} %copy-done.2, bf16[16,256]{1,0:T(8,128)(2,1)S(1)} %get-tuple-element.6.code), custom_call_target="tpu_custom_call" | custom-call | tf_op jit(solution)/shard_map/product/pallas_call | solution.py:148
  3.7 0.0 copy-start.3
  3.7 8.6 %all-gather = bf16[672,256]{1,0:T(8,128)(2,1)S(1)} all-gather(bf16[336,256]{1,0:T(8,128)(2,1)S(1)} %get-tuple-element.7.mine.message), channel_id=2, replica_groups=mesh['group'=32,'y'=2,'core'=2,'row'=4] {'core'}, dimensions={0}, use_global_device_ids=true | all-gather | bytes 516096 | tf_op jit(solution)/shard_map/all_gather | solution.py:159
  12.2 0.6 %place.1 = bf16[8,128,256]{2,1,0:T(8,128)(2,1)S(1)} custom-call(bf16[336,256]{1,0:T(8,128)(2,1)S(1)} %get-tuple-element.7.mine.message, bf16[256,256]{1,0:T(8,128)(2,1)S(1)} %get-tuple-element.8.rest, bf16[2,336,256]{2,1,0:T(8,128)(2,1)S(1)} %bitcast.1, bf16[256,256]{1,0:T(8,128)(2,1)S(1)} %get-tuple-element.9.lower), custom_call_target="tpu_custom_call" | custom-call | tf_op jit(solution)/shard_map/place/pallas_call | solution.py:160
  12.8 11.8 %all_to_all.5.pieces = bf16[8,128,256]{2,1,0:T(8,128)(2,1)S(1)} all-to-all(bf16[8,128,256]{2,1,0:T(8,128)(2,1)S(1)} %place.1), channel_id=1, replica_groups=mesh['group'=32,'y'=2,'core'=2,'row'=4] {'row','y'}, dimensions={0} | all-to-all | bytes 1048576 | tf_op jit(solution)/shard_map/all_to_all | solution.py:168
  24.6 0.0 copy-done.3
  24.6 0.7 %total.1 = (bf16[1,64,256]{2,1,0:T(8,128)(2,1)}, bf16[1,64,256]{2,1,0:T(8,128)(2,1)}) custom-call(bf16[8,128,256]{2,1,0:T(8,128)(2,1)S(1)} %all_to_all.5.pieces, bf16[336,256]{1,0:T(8,128)(2,1)S(1)} %get-tuple-element.7.mine.message, bf16[1,64,256]{2,1,0:T(8,128)(2,1)S(1)} %copy-done.3), custom_call_target="tpu_custom_call" | custom-call | tf_op jit(solution)/shard_map/total/pallas_call | solution.py:170
  (2 shorter events, 0.0 us)
Async XLA Ops:
  0.6 1.9 %copy-start.5 = (s32[1,256]{1,0:T(1,128)S(1)}, s32[1,256]{1,0:T(1,128)}, u32[]{:S(2)}) copy-start(s32[1,256]{1,0:T(1,128)} %parent_map.1) | copy-start | bytes 3076
  0.6 1.9 %copy-start.4 = (s32[1,256]{1,0:T(1,128)S(1)}, s32[1,256]{1,0:T(1,128)}, u32[]{:S(2)}) copy-start(s32[1,256]{1,0:T(1,128)} %leaf_map.1) | copy-start | bytes 3076
  0.7 2.0 %copy-start.2 = (bf16[1,64,256]{2,1,0:T(8,128)(2,1)S(1)}, bf16[1,64,256]{2,1,0:T(8,128)(2,1)}, u32[]{:S(2)}) copy-start(bf16[1,64,256]{2,1,0:T(8,128)(2,1)} %own_one.1) | copy-start | bytes 98308
  0.7 2.0 %copy-start.1 = (bf16[1,4096,256]{2,1,0:T(8,128)(2,1)S(1)}, bf16[1,4096,256]{2,1,0:T(8,128)(2,1)}, u32[]{:S(2)}) copy-start(bf16[1,4096,256]{2,1,0:T(8,128)(2,1)} %omega.1) | copy-start | bytes 6291460
  0.7 2.3 %copy-start = (bf16[1,256,4096]{2,1,0:T(8,128)(2,1)S(1)}, bf16[1,256,4096]{2,1,0:T(8,128)(2,1)}, u32[]{:S(2)}) copy-start(bf16[1,256,4096]{2,1,0:T(8,128)(2,1)} %fronts.1) | copy-start | bytes 6291460
  3.7 20.9 %copy-start.3 = (bf16[1,64,256]{2,1,0:T(8,128)(2,1)S(1)}, bf16[1,64,256]{2,1,0:T(8,128)(2,1)}, u32[]{:S(2)}) copy-start(bf16[1,64,256]{2,1,0:T(8,128)(2,1)} %own_two.1) | copy-start | bytes 98308
